TPU v7x, 32 devices: a whole 2x2x4 slice. The times are simulated.
32 devices in a mesh: dp: 2 (over x), lat: 4 (over y, core), lon: 4 (over z).
Axes of the slice: x: 2, y: 2, z: 4, core: 2. Of those that a mesh axis runs over, the one named last changes fastest.
Arguments:
- inputs: bfloat16 [2, 128, 64, 1024], P('dp', 'lat', 'lon'), may hold values from -40 to 40
- grad_out: bfloat16 [2, 128, 64, 1024], P('dp', 'lat', 'lon'), may hold values from -6 to 6
- w_qkv: bfloat16 [1024, 3072], replicated, may hold values from -0.1875 to 0.1875
Outputs:
- grad_inputs: bfloat16 [2, 128, 64, 1024], P('dp', 'lat', 'lon')
- grad_w_qkv: float32 [1024, 3072], P(('dp', 'lat', 'lon'))
All inputs are finite; a program needn't handle non-finite values.
Results may differ from a plain program's by a relative error of at most 0.011.
Values may be sent and summed in bfloat16 or wider, within the bound.
No kernel may reach another device: no remote copies, remote signals or barrier semaphores. Data moves between devices by JAX's collectives and lax.ppermute only.
A program may use at most 192 MiB of HBM per device.

v0:
```python
import jax
import jax.numpy as jnp
from jax import lax
from jax.sharding import PartitionSpec as P

HEADS = 16
WIN = 13
TILE_R = 8
TILE_C = 16
GROUP = 4


def with_halo(array, sides, width, wrap):
    for axis, dim in sides:
        size, length = (lax.axis_size(axis), array.shape[dim])
        up = [(i, (i + 1) % size) for i in range(size if wrap else size - 1)]
        down = [(j, i) for i, j in up]
        last = lax.slice_in_dim(array, length - width, length, axis=dim)
        leading = lax.slice_in_dim(array, 0, width, axis=dim)
        before = lax.ppermute(last, axis, up)
        after = lax.ppermute(leading, axis, down)
        array = jnp.concatenate([before, array, after], axis=dim)
    return array


def passed_along(block, axis, distance):
    devices = range(lax.axis_size(axis))
    route = [(i - distance, i) for i in devices if i - distance in devices]
    return lax.ppermute(block, axis, route)


def from_behind(array, axis, by):
    size = lax.axis_size(axis)
    return lax.ppermute(array, axis, [(i, (i + by) % size) for i in range(size)])


def tile_layout(row_tile, band_start, band_rows, total_rows):
    margin = WIN // 2
    first_row = band_start + row_tile * TILE_R
    window_top = jnp.clip(first_row - margin, 0, total_rows - WIN)
    region_top = jnp.minimum(window_top - band_start + margin, band_rows - TILE_R)
    query_rows = first_row + jnp.arange(TILE_R, dtype=jnp.int32)
    key_rows = region_top + band_start - margin + jnp.arange(TILE_R + WIN - 1, dtype=jnp.int32)
    return (region_top, query_rows, key_rows)


def window_mask(query_rows, key_rows, total_rows):
    margin = WIN // 2
    starts = jnp.clip(query_rows - margin, 0, total_rows - WIN)
    row_inside = (key_rows[:, None] >= starts[None, :]) & (
        key_rows[:, None] <= starts[None, :] + WIN - 1
    )
    query_cols = jnp.arange(TILE_C, dtype=jnp.int32)
    key_cols = jnp.arange(TILE_C + WIN - 1, dtype=jnp.int32)
    col_inside = (key_cols[:, None] >= query_cols[None, :]) & (
        key_cols[:, None] <= query_cols[None, :] + WIN - 1
    )
    inside = row_inside[:, None, :, None] & col_inside[None, :, None, :]
    return inside.reshape((TILE_R + WIN - 1) * (TILE_C + WIN - 1), TILE_R * TILE_C)


def tile_grads(query_tile, grad_tile, region, inside):
    query_count, width = query_tile.shape
    key_count = region.shape[0]
    head_width = width // HEADS
    norm_scale = head_width ** (-0.5)
    head_queries = query_tile.reshape(query_count, HEADS, head_width)
    head_grads = grad_tile.reshape(query_count, HEADS, head_width)
    head_keys = region[:, :width].reshape(key_count, HEADS, head_width)
    head_values = region[:, width:].reshape(key_count, HEADS, head_width)
    scores = (
        jnp.einsum("khd,ihd->hki", head_keys, head_queries, preferred_element_type=jnp.float32)
        * norm_scale
    )
    scores = jnp.where(inside[None], scores, -1e30)
    maxima = jnp.max(scores, axis=1, keepdims=True)
    exponent = jnp.exp(scores - maxima)
    attn_weights = exponent / jnp.sum(exponent, axis=1, keepdims=True)
    attn_rounded = attn_weights.astype(jnp.bfloat16)
    value_dots = jnp.einsum(
        "khd,ihd->hki", head_values, head_grads, preferred_element_type=jnp.float32
    )
    delta_terms = jnp.sum(attn_weights * value_dots, axis=1, keepdims=True)
    score_grads = (attn_weights * (value_dots - delta_terms)).astype(jnp.bfloat16)
    query_grad = (
        jnp.einsum("hki,khd->ihd", score_grads, head_keys, preferred_element_type=jnp.float32)
        * norm_scale
    )
    key_grad = (
        jnp.einsum("hki,ihd->khd", score_grads, head_queries, preferred_element_type=jnp.float32)
        * norm_scale
    )
    value_grad = jnp.einsum(
        "hki,ihd->khd", attn_rounded, head_grads, preferred_element_type=jnp.float32
    )
    region_grad = jnp.concatenate(
        [key_grad.reshape(key_count, width), value_grad.reshape(key_count, width)], axis=1
    )
    return (query_grad.reshape(query_count, width), region_grad)


def run_tiles(queries, grad_out, key_values, band_start, total_rows):
    samples, band_rows, band_cols, width = queries.shape
    region_rows = TILE_R + WIN - 1
    region_cols = TILE_C + WIN - 1
    row_tiles = band_rows // TILE_R
    col_tiles = band_cols // TILE_C
    tile_count = samples * row_tiles * col_tiles
    anchor = jnp.zeros((), jnp.int32)

    def one_tile(tile_index):
        sample = tile_index // (row_tiles * col_tiles)
        row_tile = tile_index // col_tiles % row_tiles
        col_tile = tile_index % col_tiles
        region_top, query_rows, key_rows = tile_layout(row_tile, band_start, band_rows, total_rows)
        first_col = col_tile * TILE_C
        query_tile = lax.dynamic_slice(
            queries, (sample, row_tile * TILE_R, first_col, anchor), (1, TILE_R, TILE_C, width)
        ).reshape(TILE_R * TILE_C, width)
        grad_tile = lax.dynamic_slice(
            grad_out, (sample, row_tile * TILE_R, first_col, anchor), (1, TILE_R, TILE_C, width)
        ).reshape(TILE_R * TILE_C, width)
        region = lax.dynamic_slice(
            key_values,
            (sample, region_top, first_col, anchor),
            (1, region_rows, region_cols, 2 * width),
        ).reshape(region_rows * region_cols, 2 * width)
        query_grad, region_grad = tile_grads(
            query_tile, grad_tile, region, window_mask(query_rows, key_rows, total_rows)
        )
        return (query_grad, region_grad, sample, region_top, first_col)

    def group_step(totals, group_index):
        tile_ids = group_index * GROUP + jnp.arange(GROUP, dtype=jnp.int32)
        query_grads, region_grads, sample_ids, region_tops, region_lefts = jax.vmap(one_tile)(
            tile_ids
        )
        for member in range(GROUP):
            corner = (sample_ids[member], region_tops[member], region_lefts[member], anchor)
            current = lax.dynamic_slice(totals, corner, (1, region_rows, region_cols, 2 * width))
            totals = lax.dynamic_update_slice(
                totals,
                current + region_grads[member].reshape(1, region_rows, region_cols, 2 * width),
                corner,
            )
        return (totals, query_grads)

    initial = jnp.zeros((samples, band_rows + WIN - 1, band_cols + WIN - 1, 2 * width), jnp.float32)
    totals, query_grads = lax.scan(
        group_step, initial, jnp.arange(tile_count // GROUP, dtype=jnp.int32)
    )
    query_grads = query_grads.reshape(samples, row_tiles, col_tiles, TILE_R, TILE_C, width)
    query_grads = query_grads.transpose(0, 1, 3, 2, 4, 5).reshape(
        samples, band_rows, band_cols, width
    )
    return (query_grads, totals)


def along_longitude(tensor):
    return with_halo(tensor, (("lon", 2),), WIN // 2, True)


def along_latitude(tensor):
    return with_halo(tensor, (("lat", 1),), WIN // 2, False)


def extend(tensor):
    widened = along_latitude(along_longitude(tensor))
    return widened


def give_back_latitude(totals):
    margin = WIN // 2
    extent = totals.shape[1]
    for offset in (1, -1):
        outgoing = totals[:, extent - margin :] if offset == 1 else totals[:, :margin]
        incoming = passed_along(outgoing, "lat", offset)
        if offset == 1:
            totals = totals.at[:, margin : 2 * margin].add(incoming)
        else:
            totals = totals.at[:, extent - 2 * margin : extent - margin].add(incoming)
    return totals


def give_back_longitude(totals):
    margin = WIN // 2
    extent = totals.shape[2]
    for offset in (1, -1):
        outgoing = totals[:, :, extent - margin :] if offset == 1 else totals[:, :, :margin]
        incoming = from_behind(outgoing, "lon", offset)
        if offset == 1:
            totals = totals.at[:, :, margin : 2 * margin].add(incoming)
        else:
            totals = totals.at[:, :, extent - 2 * margin : extent - margin].add(incoming)
    return totals


def body(inputs, grad_out, w_qkv):
    samples, band_rows, band_cols, width = inputs.shape
    margin = WIN // 2
    lat_count = lax.axis_size("lat")
    lon_count = lax.axis_size("lon")
    dp_count = lax.axis_size("dp")
    band_start = lax.axis_index("lat") * band_rows
    total_rows = band_rows * lat_count
    flat_inputs = inputs.reshape(-1, width)
    projected = jnp.dot(flat_inputs, w_qkv, preferred_element_type=jnp.float32).astype(jnp.bfloat16)
    projected = projected.reshape(samples, band_rows, band_cols, 3 * width)
    queries = projected[..., :width]
    key_values = extend(projected[..., width:])
    query_grads, totals = run_tiles(queries, grad_out, key_values, band_start, total_rows)
    totals = give_back_latitude(totals)[:, margin : band_rows + margin]
    totals = give_back_longitude(totals)[:, :, margin : band_cols + margin]
    grad_proj = jnp.concatenate(
        [query_grads.astype(jnp.bfloat16), totals.astype(jnp.bfloat16)], axis=-1
    ).reshape(-1, 3 * width)
    grad_inputs = lax.dot_general(
        grad_proj, w_qkv, (((1,), (1,)), ((), ())), preferred_element_type=jnp.float32
    )
    grad_inputs = grad_inputs.astype(jnp.bfloat16).reshape(inputs.shape)
    devices_all = dp_count * lat_count * lon_count
    grad_scale = float(samples * band_rows * band_cols * devices_all) ** (-0.5)
    grad_w_qkv = lax.psum_scatter(
        lax.dot_general(
            flat_inputs, grad_proj, (((0,), (0,)), ((), ())), preferred_element_type=jnp.float32
        )
        * grad_scale,
        ("dp", "lat", "lon"),
        scatter_dimension=0,
        tiled=True,
    )
    return (grad_inputs, grad_w_qkv)


def solution(mesh):
    in_specs = (P("dp", "lat", "lon", None), P("dp", "lat", "lon", None), P())
    out_specs = (P("dp", "lat", "lon", None), P(("dp", "lat", "lon"), None))
    return jax.shard_map(body, mesh=mesh, in_specs=in_specs, out_specs=out_specs, check_vma=False)
```

profile of v0, /device:TPU:0, one launch (start us, length us, event | category | flops | bytes accessed | tf_op | source)
XLA Modules:
  0.0 748.2 jit_solution(9690652242733093769)
XLA Ops:
  43.6 14.4 %collective-permute-done.1 = bf16[1,32,6,2048]{3,1,2,0:T(8,128)(2,1)} collective-permute-done((bf16[1,32,6,2048]{3,1,2,0:T(8,128)(2,1)}, bf16[1,32,6,2048]{3,1,2,0:T(8,128)(2,1)}, u32[]{:S(2)}, u32[]{:S(2)}) %collective-permute-start.1) | collective-permute-done | bytes 786464 | tf_op jit(solution)/shard_map/ppermute | solution.py:21
  101.4 19.5 %while.10 = (s32[]{:T(128)}, bf16[1,44,28,2048]{3,2,1,0:T(8,128)(2,1)}, s32[4,4]{1,0:T(4,128)S(1)}, bf16[4,1,20,28,2048]{4,3,2,1,0:T(8,128)(2,1)}, s32[]{:T(128)}) while((s32[]{:T(128)}, bf16[1,44,28,2048]{3,2,1,0:T(8,128)(2,1)}, s32[4,4]{1,0:T(4,128)S(1)}, bf16[4,1,20,28,2048]{4,3,2,1,0:T(8,128)(2,1)}, s32[]{:T(128)}) %tuple.55), condition=%wide.while_cond.4, body=%wide.while_body.4.sunk | while | flops 2 | bytes 5244009 | solution.py:123
  120.9 12.1 %copy.42 = bf16[4,1,20,28,2048]{4,0,3,2,1:T(4,128)(2,1)} copy(bf16[4,1,20,28,2048]{4,3,2,1,0:T(8,128)(2,1)} %get-tuple-element.78) | data formatting | bytes 18350080 | tf_op jit(solution)/shard_map/while/body/eval_jaxpr/vmap()/gather | solution.py:123
  133.1 10.3 %fusion.45 = (bf16[4,560,1024]{2,0,1:T(4,128)(2,1)}, bf16[4,560,1024]{2,0,1:T(4,128)(2,1)}) fusion(bf16[4,560,2048]{2,0,1:T(4,128)(2,1)} %bitcast.75), kind=kLoop, calls=%fused_computation.94 | loop fusion | bytes 18350080 | tf_op jit(solution)/shard_map/while/body/eval_jaxpr/vmap()/slice | solution.py:69
  162.5 12.5 %fusion.48 = (f32[4,16,128]{2,1,0:T(8,128)S(1)}, f32[4,16,560,128]{3,2,1,0:T(8,128)}) fusion(pred[4,560,128]{2,1,0:T(8,128)(4,1)S(1)} %copy-done.9, bf16[4,560,16,64]{1,3,2,0:T(8,128)(2,1)} %bitcast.76, bf16[4,128,16,64]{1,3,2,0:T(8,128)(2,1)S(1)} %copy-done.7), kind=kOutput, calls=%fused_computation.97 | convolution fusion | flops 605553216 | bytes 24305664 | tf_op jit(solution)/shard_map/while/body/eval_jaxpr/vmap()/sub | solution.py:77
  175.0 13.6 %fusion.3 = f32[4,16,64,560]{3,2,1,0:T(8,128)} fusion(bf16[4,128,16,64]{1,3,2,0:T(8,128)(2,1)S(1)} %copy-done.8, f32[4,16,560,128]{3,2,1,0:T(8,128)} %get-tuple-element.110, f32[4,16,128]{2,1,0:T(8,128)S(1)} %get-tuple-element.109), kind=kOutput, calls=%fused_computation.18 | convolution fusion | flops 596377600 | bytes 28606464 | tf_op jit(solution)/shard_map/while/body/eval_jaxpr/vmap(hki,ihd->khd)/dot_general | solution.py:93
  188.5 14.2 %multiply_reduce_fusion = (f32[4,16,128]{2,1,0:T(8,128)S(1)}, f32[4,16,560,128]{3,2,1,0:T(8,128)}) fusion(f32[4,16,560,128]{3,2,1,0:T(8,128)} %get-tuple-element.110, f32[4,16,128]{2,1,0:T(8,128)S(1)} %get-tuple-element.109, bf16[4,560,16,64]{1,3,2,0:T(8,128)(2,1)} %bitcast.88, bf16[4,128,16,64]{1,3,2,0:T(8,128)(2,1)S(1)} %copy-done.8), kind=kOutput, calls=%fused_computation.12 | convolution fusion | flops 600956928 | bytes 42401792 | tf_op jit(solution)/shard_map/while/body/eval_jaxpr/vmap(khd,ihd->hki)/dot_general | solution.py:80
  202.7 12.6 %multiply_convert_fusion = bf16[4,16,560,128]{3,2,1,0:T(8,128)(2,1)S(1)} fusion(f32[4,16,560,128]{3,2,1,0:T(8,128)} %get-tuple-element.112, f32[4,16,128]{2,1,0:T(8,128)S(1)} %get-tuple-element.111, f32[4,16,560,128]{3,2,1,0:T(8,128)} %get-tuple-element.110, f32[4,16,128]{2,1,0:T(8,128)S(1)} %get-tuple-element.109), kind=kLoop, calls=%fused_computation.11 | loop fusion | flops 18350080 | bytes 45940736 | tf_op jit(solution)/shard_map/while/body/eval_jaxpr/vmap()/convert_element_type | solution.py:84
  222.1 12.6 %copy.53 = f32[4,560,1024]{2,0,1:T(4,128)} copy(f32[4,560,1024]{1,2,0:T(8,128)} %bitcast.74) | data formatting | bytes 18350080 | tf_op jit(solution)/shard_map/while/body/eval_jaxpr/vmap()/reshape | solution.py:97
  234.7 12.7 %copy.54 = f32[4,560,1024]{2,0,1:T(4,128)} copy(f32[4,560,1024]{1,2,0:T(8,128)} %bitcast.84) | data formatting | bytes 18350080 | tf_op jit(solution)/shard_map/while/body/eval_jaxpr/vmap()/reshape | solution.py:97
  247.4 44.6 %pad_maximum_fusion.1 = (f32[1,560,2048]{2,0,1:T(1,128)}, f32[1,560,2048]{2,0,1:T(1,128)S(1)}, f32[1,560,2048]{2,0,1:T(1,128)}, f32[1,560,2048]{2,0,1:T(1,128)}) fusion(f32[4,560,1024]{2,0,1:T(4,128)} %copy.54, f32[4,560,1024]{2,0,1:T(4,128)} %copy.53), kind=kLoop, calls=%fused_computation.32 | loop fusion | flops 4587520 | bytes 36700160 | tf_op jit(solution)/shard_map/while/body/eval_jaxpr/vmap()/concatenate | solution.py:96
  302.7 20.9 %dynamic_update_slice.23 = f32[1,44,28,2048]{3,1,2,0:T(8,128)} dynamic-update-slice(f32[1,44,28,2048]{3,1,2,0:T(8,128)} %broadcast_in_dim.69, f32[1,20,28,2048]{3,1,2,0:T(8,128)} %copy.55, s32[]{:T(128)} %constant.234.clone.1, s32[]{:T(128)S(6)} %select_n.168, s32[]{:T(128)} %constant.234.clone.1, s32[]{:T(128)} %constant.234.clone.1) | dynamic-update-slice | bytes 9175044 | tf_op jit(solution)/shard_map/while/body/eval_jaxpr/dynamic_update_slice | solution.py:141
  323.6 10.1 %copy_add_fusion.2 = f32[1,20,28,2048]{3,1,2,0:T(8,128)} fusion(f32[1,20,28,2048]{3,0,2,1:T(1,128)} %bitcast.82, f32[1,44,28,2048]{3,1,2,0:T(8,128)} %dynamic_update_slice.23, s32[]{:T(128)S(6)} %select_n.169), kind=kLoop, calls=%fused_computation.27 | loop fusion | flops 1146880 | bytes 13762564 | tf_op jit(solution)/shard_map/while/body/eval_jaxpr/add | solution.py:143
  333.7 20.8 %dynamic_update_slice.24 = f32[1,44,28,2048]{3,1,2,0:T(8,128)} dynamic-update-slice(f32[1,44,28,2048]{3,1,2,0:T(8,128)} %dynamic_update_slice.23, f32[1,20,28,2048]{3,1,2,0:T(8,128)} %copy_add_fusion.2, s32[]{:T(128)} %constant.234.clone.1, s32[]{:T(128)S(6)} %select_n.169, s32[]{:T(128)} %constant.234.clone.1, s32[]{:T(128)} %constant.234.clone.1) | dynamic-update-slice | bytes 9175044 | tf_op jit(solution)/shard_map/while/body/eval_jaxpr/dynamic_update_slice | solution.py:141
  354.5 10.1 %copy_add_fusion.1 = f32[1,20,28,2048]{3,1,2,0:T(8,128)} fusion(f32[1,20,28,2048]{3,0,2,1:T(1,128)} %bitcast.81, f32[1,44,28,2048]{3,1,2,0:T(8,128)} %dynamic_update_slice.24, s32[]{:T(128)S(6)} %select_n.170), kind=kLoop, calls=%fused_computation.26 | loop fusion | flops 1146880 | bytes 13762564 | tf_op jit(solution)/shard_map/while/body/eval_jaxpr/add | solution.py:143
  364.6 20.2 %dynamic_update_slice.25 = f32[1,44,28,2048]{3,1,2,0:T(8,128)} dynamic-update-slice(f32[1,44,28,2048]{3,1,2,0:T(8,128)} %dynamic_update_slice.24, f32[1,20,28,2048]{3,1,2,0:T(8,128)} %copy_add_fusion.1, s32[]{:T(128)} %constant.234.clone.1, s32[]{:T(128)S(6)} %select_n.170, s32[]{:T(128)} %constant.234.clone.1, s32[]{:T(128)} %constant.234.clone.1) | dynamic-update-slice | bytes 9175044 | tf_op jit(solution)/shard_map/while/body/eval_jaxpr/dynamic_update_slice | solution.py:141
  384.8 9.6 %copy_add_fusion = f32[1,20,28,2048]{3,1,2,0:T(8,128)} fusion(f32[1,20,28,2048]{3,0,2,1:T(1,128)} %bitcast.80, f32[1,44,28,2048]{3,1,2,0:T(8,128)} %dynamic_update_slice.25, s32[]{:T(128)S(6)} %select_n.171), kind=kLoop, calls=%fused_computation.25 | loop fusion | flops 1146880 | bytes 13762564 | tf_op jit(solution)/shard_map/while/body/eval_jaxpr/add | solution.py:143
  394.4 19.7 %dynamic_update_slice.26 = f32[1,44,28,2048]{3,1,2,0:T(8,128)} dynamic-update-slice(f32[1,44,28,2048]{3,1,2,0:T(8,128)} %dynamic_update_slice.25, f32[1,20,28,2048]{3,1,2,0:T(8,128)} %copy_add_fusion, s32[]{:T(128)} %constant.234.clone.1, s32[]{:T(128)S(6)} %select_n.171, s32[]{:T(128)} %constant.234.clone.1, s32[]{:T(128)} %constant.234.clone.1) | dynamic-update-slice | bytes 9175044 | tf_op jit(solution)/shard_map/while/body/eval_jaxpr/dynamic_update_slice | solution.py:141
  440.6 17.5 %collective-permute-done.5 = f32[1,6,28,2048]{3,0,2,1:T(1,128)S(1)} collective-permute-done((f32[1,6,28,2048]{3,0,2,1:T(1,128)S(1)}, f32[1,6,28,2048]{3,0,2,1:T(1,128)S(1)}, u32[]{:S(2)}, u32[]{:S(2)}) %collective-permute-start.5) | collective-permute-done | bytes 1376288 | tf_op jit(solution)/shard_map/ppermute | solution.py:29
  461.8 10.0 %scatter-add.15 = f32[1,44,28,2048]{3,1,2,0:T(8,128)} dynamic-update-slice(f32[1,44,28,2048]{3,1,2,0:T(8,128)} %scatter-add.14, f32[1,6,28,2048]{3,1,2,0:T(8,128)} %slice_add_fusion, s32[]{:T(128)} %constant.234.clone.1, s32[]{:T(128)} %constant.239.clone.1, s32[]{:T(128)} %constant.234.clone.1, s32[]{:T(128)} %constant.234.clone.1) | dynamic-update-slice | bytes 2752516 | tf_op jit(solution)/shard_map/scatter-add | solution.py:181
  479.0 18.4 %collective-permute-done.6 = f32[1,32,6,2048]{3,1,2,0:T(8,128)S(1)} collective-permute-done((f32[1,32,6,2048]{3,1,2,0:T(8,128)S(1)}, f32[1,32,6,2048]{3,1,2,0:T(8,128)S(1)}, u32[]{:S(2)}, u32[]{:S(2)}) %collective-permute-start.6) | collective-permute-done | bytes 1572896 | tf_op jit(solution)/shard_map/ppermute | solution.py:34
  515.7 13.9 %collective-permute-done.7 = f32[1,32,6,2048]{3,1,2,0:T(8,128)} collective-permute-done((f32[1,32,6,2048]{3,1,2,0:T(8,128)}, f32[1,32,6,2048]{3,1,2,0:T(8,128)}, u32[]{:S(2)}, u32[]{:S(2)}) %collective-permute-start.7) | collective-permute-done | bytes 1572896 | tf_op jit(solution)/shard_map/ppermute | solution.py:34
  544.5 12.6 %copy.70 = f32[1024,3072]{1,0:T(8,128)} copy(f32[1024,3072]{0,1:T(8,128)} %fusion.2) | data formatting | bytes 25165824
  569.7 171.4 %reduce-scatter.4.cloned.1.call-done = f32[32,3072]{1,0:T(8,128)} async-done(((f32[1024,3072]{1,0:T(8,128)}), f32[32,3072]{1,0:T(8,128)}) %reduce-scatter.4.cloned.1.call-update) | async-done | bytes 393232
  (119 shorter events, 211.8 us)
Async XLA Ops:
  7.2 1.2 copy-start
  7.2 734.0 %reduce-scatter.4.cloned.1.call-start = ((), (), s32[]{:S(2)}) async-start(), calls=%async_computation.1 | async-start | bytes 12976128
  14.8 1.8 copy-start.5
  18.2 23.8 %collective-permute-start = (bf16[1,32,6,2048]{3,1,2,0:T(8,128)(2,1)}, bf16[1,32,6,2048]{3,1,2,0:T(8,128)(2,1)}, u32[]{:S(2)}, u32[]{:S(2)}) collective-permute-start(bf16[1,32,6,2048]{3,1,2,0:T(8,128)(2,1)} %copy.73), channel_id=1, source_target_pairs={{0,1},{1,2},{2,3},{3,0},{4,5},{5,6},{6,7},{7,4},{8,9},{9,10},{10,1... | collective-permute-start | bytes 2359304 | tf_op jit(solution)/shard_map/ppermute | solution.py:20
  22.6 35.4 %collective-permute-start.1 = (bf16[1,32,6,2048]{3,1,2,0:T(8,128)(2,1)}, bf16[1,32,6,2048]{3,1,2,0:T(8,128)(2,1)}, u32[]{:S(2)}, u32[]{:S(2)}) collective-permute-start(bf16[1,32,6,2048]{3,1,2,0:T(8,128)(2,1)} %copy.74), channel_id=1, source_target_pairs={{1,0},{2,1},{3,2},{0,3},{5,4},{6,5},{7,6},{4,7},{9,8},{10,9},{11,1... | collective-permute-start | bytes 2359304 | tf_op jit(solution)/shard_map/ppermute | solution.py:21
  43.6 16.0 %copy-start.3 = (bf16[1,32,6,2048]{3,2,1,0:T(8,128)(2,1)}, bf16[1,32,6,2048]{3,2,1,0:T(8,128)(2,1)S(1)}, u32[]{:S(2)}) copy-start(bf16[1,32,6,2048]{3,2,1,0:T(8,128)(2,1)S(1)} %copy.40) | copy-start | bytes 2359300
  59.6 1.8 copy-start.4
  61.4 34.0 %collective-permute-start.2 = (bf16[1,6,28,2048]{3,2,1,0:T(8,128)(2,1)}, bf16[1,6,28,2048]{3,2,1,0:T(8,128)(2,1)}, u32[]{:S(2)}, u32[]{:S(2)}) collective-permute-start(bf16[1,6,28,2048]{3,2,1,0:T(8,128)(2,1)} %get-tuple-element.99), channel_id=1, source_target_pairs={{0,4},{4,8},{8,12},{1,5},{5,9},{9,13},{2,6},{6,10},{10,14},{3,7},{... | collective-permute-start | bytes 2064392 | tf_op jit(solution)/shard_map/ppermute | solution.py:20
  64.2 31.2 %collective-permute-start.3 = (bf16[1,6,28,2048]{3,2,1,0:T(8,128)(2,1)}, bf16[1,6,28,2048]{3,2,1,0:T(8,128)(2,1)}, u32[]{:S(2)}, u32[]{:S(2)}) collective-permute-start(bf16[1,6,28,2048]{3,2,1,0:T(8,128)(2,1)} %get-tuple-element.100), channel_id=1, source_target_pairs={{4,0},{8,4},{12,8},{5,1},{9,5},{13,9},{6,2},{10,6},{14,10},{7,3},{... | collective-permute-start | bytes 2064392 | tf_op jit(solution)/shard_map/ppermute | solution.py:21
  152.9 9.6 %copy-start.7 = (bf16[4,128,16,64]{1,3,2,0:T(8,128)(2,1)S(1)}, bf16[4,128,16,64]{1,3,2,0:T(8,128)(2,1)}, u32[]{:S(2)}) copy-start(bf16[4,128,16,64]{1,3,2,0:T(8,128)(2,1)} %copy.46) | copy-start | bytes 3145732
  152.9 9.6 %copy-start.9 = (pred[4,560,128]{2,1,0:T(8,128)(4,1)S(1)}, pred[4,560,128]{2,1,0:T(8,128)(4,1)}, u32[]{:S(2)}) copy-start(pred[4,560,128]{2,1,0:T(8,128)(4,1)} %copy.44) | copy-start | bytes 860164
  162.4 12.5 %copy-start.8 = (bf16[4,128,16,64]{1,3,2,0:T(8,128)(2,1)S(1)}, bf16[4,128,16,64]{1,3,2,0:T(8,128)(2,1)}, u32[]{:S(2)}) copy-start(bf16[4,128,16,64]{1,3,2,0:T(8,128)(2,1)} %copy.49) | copy-start | bytes 3145732
  215.3 6.8 copy-start.1
  417.7 5.8 collective-permute-start.4
  439.3 18.8 %collective-permute-start.5 = (f32[1,6,28,2048]{3,0,2,1:T(1,128)S(1)}, f32[1,6,28,2048]{3,0,2,1:T(1,128)S(1)}, u32[]{:S(2)}, u32[]{:S(2)}) collective-permute-start(f32[1,6,28,2048]{3,0,2,1:T(1,128)S(1)} %copy.61), channel_id=1, source_target_pairs={{4,0},{8,4},{12,8},{5,1},{9,5},{13,9},{6,2},{10,6},{14,10},{7,3},{... | collective-permute-start | bytes 4128776 | tf_op jit(solution)/shard_map/ppermute | solution.py:29
  461.8 43.9 %slice-start.3 = ((s8[5242880]{0:T(1024)(128)(4,1)}), s8[1048576]{0:T(1024)(128)(4,1)S(1)}, s32[]{:S(2)}) async-start(s8[5242880]{0:T(1024)(128)(4,1)} %bitcast.77), calls=%async_computation.5 | async-start | bytes 2097152
  473.5 32.2 %slice-start.4 = ((s8[5242880]{0:T(1024)(128)(4,1)}), s8[4194304]{0:T(1024)(128)(4,1)S(1)}, s32[]{:S(2)}) async-start(s8[5242880]{0:T(1024)(128)(4,1)} %bitcast.77), calls=%async_computation.6 | async-start | bytes 8388608
  473.5 24.0 %collective-permute-start.6 = (f32[1,32,6,2048]{3,1,2,0:T(8,128)S(1)}, f32[1,32,6,2048]{3,1,2,0:T(8,128)S(1)}, u32[]{:S(2)}, u32[]{:S(2)}) collective-permute-start(f32[1,32,6,2048]{3,1,2,0:T(8,128)S(1)} %slice.284), channel_id=1, source_target_pairs={{0,1},{1,2},{2,3},{3,0},{4,5},{5,6},{6,7},{7,4},{8,9},{9,10},{10,1... | collective-permute-start | bytes 4718600 | tf_op jit(solution)/shard_map/ppermute | solution.py:34
  474.1 31.6 %slice-start = ((s8[9175040]{0:T(1024)(128)(4,1)}), s8[4194304]{0:T(1024)(128)(4,1)S(1)}, s32[]{:S(2)}) async-start(s8[9175040]{0:T(1024)(128)(4,1)} %bitcast.72), calls=%async_computation.2 | async-start | bytes 8388608
  474.1 31.6 %slice-start.1 = ((s8[9175040]{0:T(1024)(128)(4,1)}), s8[786432]{0:T(1024)(128)(4,1)S(1)}, s32[]{:S(2)}) async-start(s8[9175040]{0:T(1024)(128)(4,1)} %bitcast.72), calls=%async_computation.3 | async-start | bytes 1572864
  479.0 26.6 %slice-start.2 = ((s8[9175040]{0:T(1024)(128)(4,1)}), s8[4194304]{0:T(1024)(128)(4,1)S(1)}, s32[]{:S(2)}) async-start(s8[9175040]{0:T(1024)(128)(4,1)} %bitcast.72), calls=%async_computation.4 | async-start | bytes 8388608
  499.3 2.9 copy-start.2
  503.5 26.1 %collective-permute-start.7 = (f32[1,32,6,2048]{3,1,2,0:T(8,128)}, f32[1,32,6,2048]{3,1,2,0:T(8,128)}, u32[]{:S(2)}, u32[]{:S(2)}) collective-permute-start(f32[1,32,6,2048]{3,1,2,0:T(8,128)} %slice.286), channel_id=1, source_target_pairs={{0,3},{1,0},{2,1},{3,2},{4,7},{5,4},{6,5},{7,6},{8,11},{9,8},{10,9... | collective-permute-start | bytes 4718600 | tf_op jit(solution)/shard_map/ppermute | solution.py:34
  535.4 1.4 copy-start.6
Sparse Core Ops, SparseCore 0:
  557.2 183.8 reduce-scatter.3
where the time goes:
time: 758 us; the launch traced here: 748 us
  local copies, waits for them, and re-layouts  287 us (38%)
  waiting for transfers between devices  242 us (32%)
  other arithmetic  109 us (14%)
  matrix products  71.6 us (9%)
  between operations  21.6 us (3%)
  starting transfers between devices  16.9 us (2%)
    unnamed x2, waiting for transfers between devices  171 us
    dynamic_update_slice x4, local copies, waits for them, and re-layouts, group_step(): lax.dynamic_update_slice(totals, current + region_grads[member].reshape(1...  81.5 us
    concatenate x1, other arithmetic, tile_grads(): jnp.concatenate([key_grad.reshape(key_count, width), value_grad.reshape(k...  44.6 us
    ppermute x2, waiting for transfers between devices, from_behind(): lax.ppermute(array, axis, [(i, (i + by) % size) for i in range(size)])  32.3 us
    add x3, other arithmetic, group_step(): current + region_grads[member].reshape(1, region_rows, region_cols, 2 * w...  29.8 us
    unnamed x33, local copies, waits for them, and re-layouts  22.7 us
    ppermute x2, waiting for transfers between devices, passed_along(): return lax.ppermute(block, axis, route)  20.1 us
    slice x2, local copies, waits for them, and re-layouts, tile_grads(): head_keys = region[:, :width].reshape(key_count, HEADS, head_width)  19.8 us
  transfers between devices with their start and end apart: 9, of which 7 were waited for; matrix products, arithmetic and copies ran while one was open for 9% of the time, Pallas kernels for 0%

commit v1 on v0

v1 whole, which is shorter than its diff:
```python
import functools

import jax
import jax.numpy as jnp
from jax import lax
from jax.experimental import pallas as pl
from jax.experimental.pallas import tpu as pltpu
from jax.sharding import PartitionSpec as P

HEADS = 16
WIN = 13
MARGIN = WIN // 2
TILE_R = 4
GROUP = 4
KEY_COLS = 32
REGION_R = 16
NEG = -1e30

NT = (((1,), (1,)), ((), ()))
TN = (((0,), (0,)), ((), ()))
NN = (((1,), (0,)), ((), ()))


def dot(a, b, dims):
    return lax.dot_general(a, b, dims, preferred_element_type=jnp.float32)


def region_top(tile, band_start, band_rows, total_rows):
    lowest = jnp.where(band_start == 0, TILE_R, 0)
    highest = jnp.where(band_start + band_rows == total_rows, band_rows - 2 * TILE_R, band_rows)
    return jnp.clip(tile * TILE_R, lowest, highest)


def attention_kernel(
    band_rows, band_cols, total_rows, head_width,
    start_ref, region_ref, own_ref, grad_ref, wq_ref, wk_ref, wv_ref,
    dq_ref, top_ref, mid_ref, bottom_ref,
    mask_ref, q_ref, k_ref, v_ref, dk_ref, dv_ref,
):
    band_start = start_ref[0]
    tiles = band_rows // TILE_R
    queries = TILE_R * band_cols
    keys = REGION_R * KEY_COLS
    width = GROUP * head_width
    lanes = GROUP * queries

    @pl.when(pl.program_id(0) == 0)
    def _():
        def build(tile, carry):
            first = region_top(tile, band_start, band_rows, total_rows)
            key = lax.broadcasted_iota(jnp.int32, (keys, 2 * queries), 0)
            query = lax.broadcasted_iota(jnp.int32, (keys, 2 * queries), 1) % queries
            key_row = band_start - MARGIN + first + key // KEY_COLS
            place = key % KEY_COLS
            query_row = band_start + tile * TILE_R + query // band_cols
            query_col = query % band_cols
            window = jnp.clip(query_row - MARGIN, 0, total_rows - WIN)
            row_inside = (key_row >= window) & (key_row < window + WIN)
            key_col = jnp.where(
                place < band_cols,
                place,
                jnp.where(place < band_cols + MARGIN, place - band_cols - MARGIN, place - MARGIN),
            )
            col_inside = (jnp.abs(key_col - query_col) <= MARGIN) & (
                place < band_cols + 2 * MARGIN
            )
            mask_ref[tile] = jnp.where(row_inside & col_inside, 0.0, NEG)
            return carry

        lax.fori_loop(0, tiles, build, 0)

    q_ref[...] = (
        dot(own_ref[...], wq_ref[...], NN).astype(jnp.bfloat16) * jnp.bfloat16(head_width**-0.5)
    )
    k_ref[...] = dot(region_ref[...], wk_ref[...], NN).astype(jnp.bfloat16)
    v_ref[...] = dot(region_ref[...], wv_ref[...], NN).astype(jnp.bfloat16)
    dk_ref[...] = jnp.zeros_like(dk_ref)
    dv_ref[...] = jnp.zeros_like(dv_ref)

    def spread(rows):
        block = jnp.concatenate([rows] * GROUP, axis=0)
        head_row = lax.broadcasted_iota(jnp.int32, (lanes, width), 0) // queries
        head_col = lax.broadcasted_iota(jnp.int32, (lanes, width), 1) // head_width
        return jnp.where(head_row == head_col, block, jnp.zeros_like(block))

    def one_tile(tile, carry):
        first = region_top(tile, band_start, band_rows, total_rows)
        region = pl.ds(pl.multiple_of(first * KEY_COLS, TILE_R * KEY_COLS), keys)
        mine = pl.ds(pl.multiple_of(tile * queries, queries), queries)
        q_wide = spread(q_ref[mine, :])
        g_wide = spread(grad_ref[mine, :])
        mask = mask_ref[tile]
        scores = dot(k_ref[region, :], q_wide, NT) + jnp.concatenate([mask, mask], axis=1)
        dots = dot(v_ref[region, :], g_wide, NT)
        exponent = jnp.exp(scores - jnp.max(scores, axis=0, keepdims=True))
        inverse = 1.0 / jnp.sum(exponent, axis=0, keepdims=True)
        attn = exponent * inverse
        delta = jnp.sum(attn * dots, axis=0, keepdims=True)
        dscore = (attn * (dots - delta)).astype(jnp.bfloat16)
        dv_ref[region, :] += dot(attn.astype(jnp.bfloat16), g_wide, NN)
        dk_ref[region, :] += dot(dscore, q_wide, NN)
        dq_wide = dot(dscore, k_ref[region, :], TN)
        head_col = lax.broadcasted_iota(jnp.int32, (queries, width), 1) // head_width
        dq = jnp.zeros((queries, width), jnp.float32)
        for head in range(GROUP):
            dq = jnp.where(head_col == head, dq_wide[head * queries : (head + 1) * queries], dq)
        dq_ref[mine, :] = (dq * head_width**-0.5).astype(jnp.bfloat16)
        return carry

    lax.fori_loop(0, tiles, one_tile, 0)

    edge = MARGIN * KEY_COLS
    inner = band_rows * KEY_COLS
    for part, total in enumerate((dk_ref, dv_ref)):
        top_ref[part] = total[:edge, :].astype(jnp.bfloat16)
        mid_ref[part] = total[edge : edge + inner, :].astype(jnp.bfloat16)
        bottom_ref[part] = total[edge + inner :, :].astype(jnp.bfloat16)


def attention_grads(region, own, grad_out, w_qkv, band_start, band_rows, band_cols, total_rows):
    tokens, width = own.shape
    head_width = width // HEADS
    block = GROUP * head_width
    groups = HEADS // GROUP
    edge = MARGIN * KEY_COLS
    inner = band_rows * KEY_COLS
    region_tokens = inner + 2 * edge
    tiles = band_rows // TILE_R
    queries = TILE_R * band_cols
    keys = REGION_R * KEY_COLS
    whole = lambda g: (0, 0)
    return pl.pallas_call(
        functools.partial(attention_kernel, band_rows, band_cols, total_rows, head_width),
        grid=(groups,),
        in_specs=[
            pl.BlockSpec(memory_space=pltpu.SMEM),
            pl.BlockSpec((region_tokens, width), whole),
            pl.BlockSpec((tokens, width), whole),
            pl.BlockSpec((tokens, block), lambda g: (0, g)),
            pl.BlockSpec((width, block), lambda g: (0, g)),
            pl.BlockSpec((width, block), lambda g: (0, groups + g)),
            pl.BlockSpec((width, block), lambda g: (0, 2 * groups + g)),
        ],
        out_specs=[
            pl.BlockSpec((tokens, block), lambda g: (0, g)),
            pl.BlockSpec((2, edge, block), lambda g: (0, 0, g)),
            pl.BlockSpec((2, inner, block), lambda g: (0, 0, g)),
            pl.BlockSpec((2, edge, block), lambda g: (0, 0, g)),
        ],
        out_shape=[
            jax.ShapeDtypeStruct((tokens, width), jnp.bfloat16),
            jax.ShapeDtypeStruct((2, edge, width), jnp.bfloat16),
            jax.ShapeDtypeStruct((2, inner, width), jnp.bfloat16),
            jax.ShapeDtypeStruct((2, edge, width), jnp.bfloat16),
        ],
        scratch_shapes=[
            pltpu.VMEM((tiles, keys, 2 * queries), jnp.float32),
            pltpu.VMEM((tokens, block), jnp.bfloat16),
            pltpu.VMEM((region_tokens, block), jnp.bfloat16),
            pltpu.VMEM((region_tokens, block), jnp.bfloat16),
            pltpu.VMEM((region_tokens, block), jnp.float32),
            pltpu.VMEM((region_tokens, block), jnp.float32),
        ],
        compiler_params=pltpu.CompilerParams(
            dimension_semantics=("arbitrary",), vmem_limit_bytes=50 * 1024 * 1024
        ),
    )(band_start.reshape(1), region, own, grad_out, w_qkv, w_qkv, w_qkv)


def shifted(array, axis, by, wrap):
    size = lax.axis_size(axis)
    route = [(i, (i + by) % size) for i in range(size) if wrap or 0 <= i + by < size]
    return lax.ppermute(array, axis, route)


def body(inputs, grad_out, w_qkv):
    _, band_rows, band_cols, width = inputs.shape
    lat_count = lax.axis_size("lat")
    devices_all = lat_count * lax.axis_size("lon") * lax.axis_size("dp")
    band_start = lax.axis_index("lat") * band_rows
    total_rows = band_rows * lat_count
    tokens = band_rows * band_cols
    own = inputs.reshape(band_rows, band_cols, width)
    flat_inputs = inputs.reshape(tokens, width)

    left = shifted(own[:, band_cols - MARGIN :], "lon", 1, True)
    right = shifted(own[:, :MARGIN], "lon", -1, True)
    pad = jnp.zeros((band_rows, KEY_COLS - band_cols - 2 * MARGIN, width), own.dtype)
    middle = jnp.concatenate([own, left, right, pad], axis=1)
    above = shifted(middle[band_rows - MARGIN :], "lat", 1, False)
    below = shifted(middle[:MARGIN], "lat", -1, False)
    region = jnp.concatenate([above, middle, below], axis=0)
    region = region.reshape(-1, width)

    dq, top, mid, bottom = attention_grads(
        region, flat_inputs, grad_out.reshape(tokens, width), w_qkv,
        band_start, band_rows, band_cols, total_rows,
    )
    from_below = shifted(top, "lat", -1, False)
    from_above = shifted(bottom, "lat", 1, False)
    edge = MARGIN * KEY_COLS
    mid = mid.astype(jnp.float32)
    mid = mid.at[:, :edge].add(from_above.astype(jnp.float32))
    mid = mid.at[:, mid.shape[1] - edge :].add(from_below.astype(jnp.float32))
    mid = mid.reshape(2, band_rows, KEY_COLS, width)
    to_left = mid[:, :, band_cols : band_cols + MARGIN].astype(jnp.bfloat16)
    to_right = mid[:, :, band_cols + MARGIN : band_cols + 2 * MARGIN].astype(jnp.bfloat16)
    from_right = shifted(to_left, "lon", -1, True)
    from_left = shifted(to_right, "lon", 1, True)
    mid = mid[:, :, :band_cols]
    mid = mid.at[:, :, :MARGIN].add(from_left.astype(jnp.float32))
    mid = mid.at[:, :, band_cols - MARGIN :].add(from_right.astype(jnp.float32))
    dkv = mid.astype(jnp.bfloat16).reshape(2, tokens, width)
    grad_proj = jnp.concatenate([dq, dkv[0], dkv[1]], axis=-1)
    grad_inputs = dot(grad_proj, w_qkv, NT).astype(jnp.bfloat16).reshape(inputs.shape)
    grad_scale = float(tokens * devices_all) ** -0.5
    grad_w = (dot(flat_inputs, grad_proj, TN) * grad_scale).astype(jnp.bfloat16)
    grad_w = lax.psum_scatter(grad_w, ("dp", "lat", "lon"), scatter_dimension=0, tiled=True)
    return (grad_inputs, grad_w.astype(jnp.float32))


def solution(mesh):
    in_specs = (P("dp", "lat", "lon", None), P("dp", "lat", "lon", None), P())
    out_specs = (P("dp", "lat", "lon", None), P(("dp", "lat", "lon"), None))
    return jax.shard_map(body, mesh=mesh, in_specs=in_specs, out_specs=out_specs, check_vma=False)
```

time: 758 us -> 286 us (0.38); the launches traced: 748 us -> 286 us
  local copies, waits for them, and re-layouts: 287 us -> 26 us
  other arithmetic: 109 us -> 10.5 us
  waiting for transfers between devices: 242 us -> 160 us
  matrix products: 71.6 us -> 13.5 us
  Pallas kernels: 0 us -> 40.9 us
    dynamic_update_slice x4 -> x0, local copies, waits for them, and re-layouts: 81.5 us -> none  [group_step(): lax.dynamic_update_slice(totals, current + region_grads[member].reshape(1...]
    unnamed x2, waiting for transfers between devices: 171 us -> 105 us
    slice x16 -> x6, local copies, waits for them, and re-layouts: 54.3 us -> 3.5 us  [the longest x1 1.46 us: body(): left = shifted(own[:, band_cols - MARGIN:], 'lon', 1, True)]
    concatenate x4 -> x1, other arithmetic: 50.9 us -> 3.51 us  [body(): region = jnp.concatenate([above, middle, below], axis=0)]
    dot_general x7 -> x2, matrix products: 59 us -> 13.5 us  [dot(): return lax.dot_general(a, b, dims, preferred_element_type=jnp.float32)]
    pallas_call x0 -> x1, Pallas kernels: none -> 40.9 us  [attention_grads(): pl.pallas_call(functools.partial(attention_kernel, band_rows, band_cols,...]
    gather x15 -> x0, local copies, waits for them, and re-layouts: 37.3 us -> none
    add x7 -> x0, other arithmetic: 36.8 us -> none  [the longest x3 29.8 us: group_step(): current + region_grads[member].reshape(1, region_rows, region_cols, 2 * w...]
  transfers between devices with their start and end apart: 9 -> 9, of which waited for: 7 -> 7; matrix products, arithmetic and copies ran while one was open for 9% -> 6% of each run, Pallas kernels for 0% -> 0%
where the time goes in v1:
time: 286 us
  waiting for transfers between devices  160 us (56%)
  Pallas kernels  40.9 us (14%)
  local copies, waits for them, and re-layouts  26 us (9%)
  starting transfers between devices  20.9 us (7%)
  between operations  14.2 us (5%)
  matrix products  13.5 us (5%)
  other arithmetic  10.5 us (4%)
    unnamed x2, waiting for transfers between devices  105 us
    ppermute x8, waiting for transfers between devices, shifted(): return lax.ppermute(array, axis, route)  54.7 us
    pallas_call x1, Pallas kernels, attention_grads(): pl.pallas_call(functools.partial(attention_kernel, band_rows, band_cols,...  40.9 us
    ppermute x8, starting transfers between devices, shifted(): return lax.ppermute(array, axis, route)  20.8 us
    dot_general x2, matrix products, dot(): return lax.dot_general(a, b, dims, preferred_element_type=jnp.float32)  13.5 us
    unnamed x9, local copies, waits for them, and re-layouts  13.1 us
    reshape x2, local copies, waits for them, and re-layouts, body(): mid = mid.reshape(2, band_rows, KEY_COLS, width)  9.31 us
  transfers between devices with their start and end apart: 9, of which 7 were waited for; matrix products, arithmetic and copies ran while one was open for 6% of the time, Pallas kernels for 0%

profile of v1, /device:TPU:0, one launch (start us, length us, event | category | flops | bytes accessed | tf_op | source)
XLA Modules:
  0.0 285.7 jit_solution(8248758875138171754)
XLA Ops:
  7.2 1.5 fusion.9
  8.7 3.1 %collective-permute-start = (bf16[32,6,1024]{2,1,0:T(8,128)(2,1)S(1)}, bf16[32,6,1024]{2,1,0:T(8,128)(2,1)S(1)}, u32[]{:S(2)}, u32[]{:S(2)}) collective-permute-start(bf16[32,6,1024]{2,1,0:T(8,128)(2,1)S(1)} %get-tuple-element.68), channel_id=1, source_target_pairs={{0,1},{1,2},{2,3},{3,0},{4,5},{5,6},{6,7},{7,4},{8,9},{9,10},{10,1... | collective-permute-start | bytes 1179656 | tf_op jit(solution)/shard_map/ppermute | solution.py:173
  11.8 2.1 collective-permute-start.1
  13.9 12.7 %collective-permute-done = bf16[32,6,1024]{2,1,0:T(8,128)(2,1)S(1)} collective-permute-done((bf16[32,6,1024]{2,1,0:T(8,128)(2,1)S(1)}, bf16[32,6,1024]{2,1,0:T(8,128)(2,1)S(1)}, u32[]{:S(2)}, u32[]{:S(2)}) %collective-permute-start) | collective-permute-done | bytes 393248 | tf_op jit(solution)/shard_map/ppermute | solution.py:173
  26.6 9.8 %collective-permute-done.1 = bf16[32,6,1024]{2,1,0:T(8,128)(2,1)S(1)} collective-permute-done((bf16[32,6,1024]{2,1,0:T(8,128)(2,1)S(1)}, bf16[32,6,1024]{2,1,0:T(8,128)(2,1)S(1)}, u32[]{:S(2)}, u32[]{:S(2)}) %collective-permute-start.1) | collective-permute-done | bytes 393248 | tf_op jit(solution)/shard_map/ppermute | solution.py:173
  36.5 2.0 pad_maximum_fusion.7
  38.4 1.3 collective-permute-start.2
  39.8 1.3 collective-permute-start.3
  41.3 4.0 %collective-permute-done.3 = bf16[6,32,1024]{2,1,0:T(8,128)(2,1)} collective-permute-done((bf16[6,32,1024]{2,1,0:T(8,128)(2,1)S(1)}, bf16[6,32,1024]{2,1,0:T(8,128)(2,1)}, u32[]{:S(2)}, u32[]{:S(2)}) %collective-permute-start.3) | collective-permute-done | bytes 393248 | tf_op jit(solution)/shard_map/ppermute | solution.py:173
  45.2 3.5 %pad_maximum_fusion.1 = bf16[44,32,1024]{2,1,0:T(8,128)(2,1)} fusion(bf16[6,32,1024]{2,1,0:T(8,128)(2,1)} %collective-permute-done.3, bf16[32,4,1024]{2,1,0:T(4,128)(2,1)S(1)} %broadcast_in_dim.3, bf16[32,6,1024]{2,1,0:T(8,128)(2,1)S(1)} %collective-permute-done.1, bf16[32,6,1024]{2,1,0:T(8,128)(2,1)S(1)} %collective-permute-done, ...), kind=kLoop, calls=%fused_computation.3 | loop fusion | flops 17301504 | bytes 5767168 | tf_op jit(solution)/shard_map/concatenate | solution.py:192
  48.7 40.9 %shard_map.50 = (bf16[512,1024]{1,0:T(8,128)(2,1)S(1)}, bf16[2,192,1024]{2,1,0:T(8,128)(2,1)S(1)}, bf16[2,1024,1024]{2,1,0:T(8,128)(2,1)}, bf16[2,192,1024]{2,1,0:T(8,128)(2,1)S(1)}) custom-call(s32[1]{0:T(128)} %bitcast.start_ref, bf16[1408,1024]{1,0:T(8,128)(2,1)} %bitcast.21, bf16[512,1024]{1,0:T(8,128)(2,1)S(1)} %bitcast.17, bf16[512,1024]{1,0:T(8,128)(2,1)} %bitcast.22, ...), custom_call_target="tpu_custom_call" | custom-call | tf_op jit(solution)/shard_map/pallas_call | solution.py:132
  89.6 7.9 %collective-permute-start.4 = (bf16[2,192,1024]{2,1,0:T(8,128)(2,1)S(1)}, bf16[2,192,1024]{2,1,0:T(8,128)(2,1)S(1)}, u32[]{:S(2)}, u32[]{:S(2)}) collective-permute-start(bf16[2,192,1024]{2,1,0:T(8,128)(2,1)S(1)} %get-tuple-element.56), channel_id=1, source_target_pairs={{0,4},{4,8},{8,12},{1,5},{5,9},{9,13},{2,6},{6,10},{10,14},{3,7},{... | collective-permute-start | bytes 2359304 | tf_op jit(solution)/shard_map/ppermute | solution.py:173
  97.5 1.3 collective-permute-start.5
  98.8 3.2 %convert_element_type.32 = f32[2,1024,1024]{2,1,0:T(8,128)S(1)} convert(bf16[2,1024,1024]{2,1,0:T(8,128)(2,1)} %get-tuple-element.55) | non-fusion elementwise | flops 2097152 | bytes 12582912 | tf_op jit(solution)/shard_map/convert_element_type | solution.py:202
  102.9 4.5 %copy.15 = bf16[2,32,32,1024]{3,1,2,0:T(8,128)(2,1)S(1)} copy(f32[2,32,32,1024]{3,2,1,0:T(8,128)S(1)} %bitcast.19) | data formatting | bytes 12582912 | tf_op jit(solution)/shard_map/reshape | solution.py:205
  108.7 2.7 collective-permute-start.7
  111.4 4.9 %copy.6 = f32[2,32,32,1024]{3,1,2,0:T(8,128)S(1)} copy(f32[2,32,32,1024]{3,2,1,0:T(8,128)S(1)} %bitcast.20) | data formatting | bytes 16777216 | tf_op jit(solution)/shard_map/reshape | solution.py:205
  116.8 5.8 %collective-permute-done.6 = bf16[2,32,6,1024]{3,1,2,0:T(8,128)(2,1)S(1)} collective-permute-done((bf16[2,32,6,1024]{3,1,2,0:T(8,128)(2,1)S(1)}, bf16[2,32,6,1024]{3,1,2,0:T(8,128)(2,1)S(1)}, u32[]{:S(2)}, u32[]{:S(2)}) %collective-permute-start.6) | collective-permute-done | bytes 786464 | tf_op jit(solution)/shard_map/ppermute | solution.py:173
  122.9 22.2 %collective-permute-done.7 = bf16[2,32,6,1024]{3,1,2,0:T(8,128)(2,1)S(1)} collective-permute-done((bf16[2,32,6,1024]{3,1,2,0:T(8,128)(2,1)S(1)}, bf16[2,32,6,1024]{3,1,2,0:T(8,128)(2,1)S(1)}, u32[]{:S(2)}, u32[]{:S(2)}) %collective-permute-start.7) | collective-permute-done | bytes 786464 | tf_op jit(solution)/shard_map/ppermute | solution.py:173
  148.2 6.3 %fusion = bf16[1024,3072]{0,1:T(8,128)(2,1)} fusion(bf16[512,1024]{1,0:T(8,128)(2,1)S(1)} %bitcast.18, bf16[512,1024]{1,0:T(8,128)(2,1)S(1)} %bitcast.25, bf16[512,1024]{1,0:T(8,128)(2,1)S(1)} %bitcast.23, bf16[512,1024]{1,0:T(8,128)(2,1)S(1)} %get-tuple-element.54), kind=kOutput, calls=%fused_computation.1 | convolution fusion | flops 3236954112 | bytes 10485760 | tf_op jit(solution)/shard_map/dot_general | solution.py:25
  154.5 8.7 %copy.12 = bf16[1024,3072]{1,0:T(8,128)(2,1)} copy(bf16[1024,3072]{0,1:T(8,128)(2,1)} %fusion) | data formatting | bytes 12582912
  164.4 7.2 %convolution_convert_fusion = bf16[512,1024]{1,0:T(8,128)(2,1)} fusion(bf16[1024,3072]{1,0:T(8,128)(2,1)} %wv_ref.1, bf16[512,1024]{1,0:T(8,128)(2,1)S(1)} %bitcast.26, bf16[512,1024]{1,0:T(8,128)(2,1)S(1)} %bitcast.24, bf16[512,1024]{1,0:T(8,128)(2,1)S(1)} %get-tuple-element.54), kind=kOutput, calls=%fused_computation.12 | convolution fusion | flops 3231186944 | bytes 10485760 | tf_op jit(solution)/shard_map/dot_general | solution.py:25
  171.6 104.9 %reduce-scatter.4.cloned.1.call-done = bf16[32,3072]{1,0:T(8,128)(2,1)} async-done(((bf16[1024,3072]{1,0:T(8,128)(2,1)}), bf16[32,3072]{1,0:T(8,128)(2,1)}) %reduce-scatter.4.cloned.1.call-update) | async-done | bytes 196624
  276.5 1.3 copy.13
  (24 shorter events, 8.6 us)
Async XLA Ops:
  7.2 38.1 %copy-start = (bf16[1,32,16,1024]{3,2,1,0:T(8,128)(2,1)S(1)}, bf16[1,32,16,1024]{3,2,1,0:T(8,128)(2,1)}, u32[]{:S(2)}) copy-start(bf16[1,32,16,1024]{3,2,1,0:T(8,128)(2,1)} %param.11) | copy-start | bytes 3145732
  7.2 269.3 %reduce-scatter.4.cloned.1.call-start = ((), (), s32[]{:S(2)}) async-start(), calls=%async_computation.1 | async-start | bytes 6488064
  8.7 17.9 %collective-permute-start = (bf16[32,6,1024]{2,1,0:T(8,128)(2,1)S(1)}, bf16[32,6,1024]{2,1,0:T(8,128)(2,1)S(1)}, u32[]{:S(2)}, u32[]{:S(2)}) collective-permute-start(bf16[32,6,1024]{2,1,0:T(8,128)(2,1)S(1)} %get-tuple-element.68), channel_id=1, source_target_pairs={{0,1},{1,2},{2,3},{3,0},{4,5},{5,6},{6,7},{7,4},{8,9},{9,10},{10,1... | collective-permute-start | bytes 1179656 | tf_op jit(solution)/shard_map/ppermute | solution.py:173
  11.8 24.6 %collective-permute-start.1 = (bf16[32,6,1024]{2,1,0:T(8,128)(2,1)S(1)}, bf16[32,6,1024]{2,1,0:T(8,128)(2,1)S(1)}, u32[]{:S(2)}, u32[]{:S(2)}) collective-permute-start(bf16[32,6,1024]{2,1,0:T(8,128)(2,1)S(1)} %get-tuple-element.69), channel_id=1, source_target_pairs={{0,3},{1,0},{2,1},{3,2},{4,7},{5,4},{6,5},{7,6},{8,11},{9,8},{10,9... | collective-permute-start | bytes 1179656 | tf_op jit(solution)/shard_map/ppermute | solution.py:173
  38.4 2.8 collective-permute-start.2
  39.8 5.5 %collective-permute-start.3 = (bf16[6,32,1024]{2,1,0:T(8,128)(2,1)S(1)}, bf16[6,32,1024]{2,1,0:T(8,128)(2,1)}, u32[]{:S(2)}, u32[]{:S(2)}) collective-permute-start(bf16[6,32,1024]{2,1,0:T(8,128)(2,1)S(1)} %get-tuple-element.65), channel_id=1, source_target_pairs={{4,0},{8,4},{12,8},{5,1},{9,5},{13,9},{6,2},{10,6},{14,10},{7,3},{... | collective-permute-start | bytes 1179656 | tf_op jit(solution)/shard_map/ppermute | solution.py:173
  89.6 12.4 %collective-permute-start.4 = (bf16[2,192,1024]{2,1,0:T(8,128)(2,1)S(1)}, bf16[2,192,1024]{2,1,0:T(8,128)(2,1)S(1)}, u32[]{:S(2)}, u32[]{:S(2)}) collective-permute-start(bf16[2,192,1024]{2,1,0:T(8,128)(2,1)S(1)} %get-tuple-element.56), channel_id=1, source_target_pairs={{0,4},{4,8},{8,12},{1,5},{5,9},{9,13},{2,6},{6,10},{10,14},{3,7},{... | collective-permute-start | bytes 2359304 | tf_op jit(solution)/shard_map/ppermute | solution.py:173
  97.5 5.0 %collective-permute-start.5 = (bf16[2,192,1024]{2,1,0:T(8,128)(2,1)S(1)}, bf16[2,192,1024]{2,1,0:T(8,128)(2,1)S(1)}, u32[]{:S(2)}, u32[]{:S(2)}) collective-permute-start(bf16[2,192,1024]{2,1,0:T(8,128)(2,1)S(1)} %get-tuple-element.57), channel_id=1, source_target_pairs={{4,0},{8,4},{12,8},{5,1},{9,5},{13,9},{6,2},{10,6},{14,10},{7,3},{... | collective-permute-start | bytes 2359304 | tf_op jit(solution)/shard_map/ppermute | solution.py:173
  107.6 15.1 %collective-permute-start.6 = (bf16[2,32,6,1024]{3,1,2,0:T(8,128)(2,1)S(1)}, bf16[2,32,6,1024]{3,1,2,0:T(8,128)(2,1)S(1)}, u32[]{:S(2)}, u32[]{:S(2)}) collective-permute-start(bf16[2,32,6,1024]{3,1,2,0:T(8,128)(2,1)S(1)} %get-tuple-element.63), channel_id=1, source_target_pairs={{0,1},{1,2},{2,3},{3,0},{4,5},{5,6},{6,7},{7,4},{8,9},{9,10},{10,1... | collective-permute-start | bytes 2359304 | tf_op jit(solution)/shard_map/ppermute | solution.py:173
  108.7 36.4 %collective-permute-start.7 = (bf16[2,32,6,1024]{3,1,2,0:T(8,128)(2,1)S(1)}, bf16[2,32,6,1024]{3,1,2,0:T(8,128)(2,1)S(1)}, u32[]{:S(2)}, u32[]{:S(2)}) collective-permute-start(bf16[2,32,6,1024]{3,1,2,0:T(8,128)(2,1)S(1)} %get-tuple-element.62), channel_id=1, source_target_pairs={{0,3},{1,0},{2,1},{3,2},{4,7},{5,4},{6,5},{7,6},{8,11},{9,8},{10,9... | collective-permute-start | bytes 2359304 | tf_op jit(solution)/shard_map/ppermute | solution.py:173
  147.2 1.0 copy-start.1
  163.1 1.2 copy-start.2
Sparse Core Ops, SparseCore 0:
  163.3 113.1 reduce-scatter.3

commit v2 on v1

v2 whole, which is shorter than its diff:
```python
import functools

import jax
import jax.numpy as jnp
import numpy as np
from jax import lax
from jax.experimental import pallas as pl
from jax.experimental.pallas import tpu as pltpu
from jax.sharding import PartitionSpec as P

HEADS = 16
WIN = 13
MARGIN = WIN // 2
TILE_R = 4
GROUP = 4
KEY_COLS = 32
HALO_COLS = 16
REGION_R = 16
PAD_R = 2
EDGE_R = MARGIN + PAD_R
NEG = -1e30
BF = jnp.bfloat16
F32 = jnp.float32
MIB = 1024 * 1024
LANES = 128

NT = (((1,), (1,)), ((), ()))
TN = (((0,), (0,)), ((), ()))
NN = (((1,), (0,)), ((), ()))


def dot(a, b, dims=NN):
    return lax.dot_general(a, b, dims, preferred_element_type=F32)


def region_top(tile, band_start, band_rows, total_rows):
    lowest = jnp.where(band_start == 0, TILE_R, 0)
    highest = jnp.where(band_start + band_rows == total_rows, band_rows - 2 * TILE_R, band_rows)
    return jnp.clip(tile * TILE_R, lowest, highest)


def mask_kernel(band_rows, band_cols, total_rows, start_ref, mask_ref):
    band_start = start_ref[0]
    tile = pl.program_id(0)
    shape = mask_ref.shape[1:]
    first = region_top(tile, band_start, band_rows, total_rows)
    key = lax.broadcasted_iota(jnp.int32, shape, 0)
    query = lax.broadcasted_iota(jnp.int32, shape, 1) % (TILE_R * band_cols)
    key_row = band_start - MARGIN + first + key // KEY_COLS
    place = key % KEY_COLS
    query_row = band_start + tile * TILE_R + query // band_cols
    query_col = query % band_cols
    window = jnp.clip(query_row - MARGIN, 0, total_rows - WIN)
    row_inside = (key_row >= window) & (key_row < window + WIN)
    key_col = jnp.where(
        place < band_cols,
        place,
        jnp.where(place < band_cols + MARGIN, place - band_cols - MARGIN, place - MARGIN),
    )
    col_inside = (jnp.abs(key_col - query_col) <= MARGIN) & (place < band_cols + 2 * MARGIN)
    mask_ref[0] = jnp.where(row_inside & col_inside, 0.0, NEG).astype(BF)


def window_masks(start, band_rows, band_cols, total_rows):
    tiles = band_rows // TILE_R
    shape = (REGION_R * KEY_COLS, 2 * TILE_R * band_cols)
    return pl.pallas_call(
        functools.partial(mask_kernel, band_rows, band_cols, total_rows),
        grid=(tiles,),
        in_specs=[pl.BlockSpec(memory_space=pltpu.SMEM)],
        out_specs=pl.BlockSpec((1,) + shape, lambda t: (t, 0, 0)),
        out_shape=jax.ShapeDtypeStruct((tiles,) + shape, BF),
        cost_estimate=pl.CostEstimate(flops=10**7, bytes_accessed=2**21, transcendentals=0),
    )(start)


def attention_kernel(band_rows, band_cols, total_rows, head_width, aliased, *refs):
    (start_ref, mask_ref, left_ref, right_ref, above_ref, below_ref, cl_ref, cr_ref,
     oq_ref, ok_ref, ov_ref, grad_ref, wk_ref, wv_ref) = refs[:14]
    (dq_ref, top_ref, bottom_ref, mid_ref, to_left_ref, to_right_ref,
     halo_ref, spot_ref, q_ref, k_ref, v_ref, dk_ref, dv_ref) = refs[14 + aliased :]
    band_start = start_ref[0]
    tiles = band_rows // TILE_R
    queries = TILE_R * band_cols
    keys = REGION_R * KEY_COLS
    width = GROUP * head_width
    lanes = GROUP * queries
    region_rows = band_rows + 2 * MARGIN
    side = MARGIN * band_rows
    edge = MARGIN * band_cols
    corner = 2 * MARGIN * MARGIN
    at_above = 2 * side
    at_below = at_above + edge
    at_cl = at_below + edge
    at_cr = at_cl + -(-corner // 16) * 16
    halves = [(i, slice(i * LANES, (i + 1) * LANES)) for i in range(width // LANES)]

    @pl.when(pl.program_id(0) == 0)
    def _():
        halo_ref[:side] = left_ref[...]
        halo_ref[side:at_above] = right_ref[...]
        halo_ref[at_above:at_below] = above_ref[...]
        halo_ref[at_below:at_cl] = below_ref[...]
        halo_ref[at_cl : at_cl + corner] = cl_ref[...]
        halo_ref[at_cr : at_cr + corner] = cr_ref[...]
        spot_ref[...] = jnp.zeros_like(spot_ref)

    def place(target, own, weights):
        fresh = dot(halo_ref[...], weights)
        for col in range(MARGIN):
            start = MARGIN * HALO_COLS + col
            for part, at in halves:
                spot_ref[part, pl.ds(start, band_rows, stride=HALO_COLS), :] = fresh[
                    col * band_rows : (col + 1) * band_rows, at
                ]
                spot_ref[part, pl.ds(start + MARGIN, band_rows, stride=HALO_COLS), :] = fresh[
                    side + col * band_rows : side + (col + 1) * band_rows, at
                ]
        for row in range(2 * MARGIN):
            spot = (row if row < MARGIN else row + band_rows) * HALO_COLS
            for part, at in halves:
                spot_ref[part, spot : spot + MARGIN, :] = fresh[
                    at_cl + row * MARGIN : at_cl + (row + 1) * MARGIN, at
                ]
                spot_ref[part, spot + MARGIN : spot + 2 * MARGIN, :] = fresh[
                    at_cr + row * MARGIN : at_cr + (row + 1) * MARGIN, at
                ]
        for row in range(region_rows):
            base = row * KEY_COLS
            inner = row - MARGIN
            if inner < 0:
                ours = fresh[at_above + row * band_cols : at_above + (row + 1) * band_cols].astype(BF)
            elif inner < band_rows:
                ours = own[inner * band_cols : (inner + 1) * band_cols, :]
            else:
                past = at_below + (inner - band_rows) * band_cols
                ours = fresh[past : past + band_cols].astype(BF)
            target[base : base + band_cols, :] = ours
            for part, at in halves:
                target[base + band_cols : base + KEY_COLS, at] = spot_ref[
                    part, row * HALO_COLS : (row + 1) * HALO_COLS, :
                ].astype(BF)

    place(k_ref, ok_ref, wk_ref[...])
    place(v_ref, ov_ref, wv_ref[...])
    q_ref[...] = oq_ref[...] * BF(head_width**-0.5)
    dk_ref[...] = jnp.zeros_like(dk_ref)
    dv_ref[...] = jnp.zeros_like(dv_ref)

    def spread(rows):
        block = jnp.concatenate([rows] * GROUP, axis=0)
        head_row = lax.broadcasted_iota(jnp.int32, (lanes, width), 0) // queries
        head_col = lax.broadcasted_iota(jnp.int32, (lanes, width), 1) // head_width
        return jnp.where(head_row == head_col, block, jnp.zeros_like(block))

    def one_tile(tile, carry):
        first = region_top(tile, band_start, band_rows, total_rows)
        region = pl.ds(pl.multiple_of(first * KEY_COLS, TILE_R * KEY_COLS), keys)
        total = pl.ds(pl.multiple_of((first + PAD_R) * KEY_COLS, PAD_R * KEY_COLS), keys)
        mine = pl.ds(pl.multiple_of(tile * queries, queries), queries)
        q_wide = spread(q_ref[mine, :])
        g_wide = spread(grad_ref[mine, :])
        mask = mask_ref[tile].astype(F32)
        scores = dot(k_ref[region, :], q_wide, NT) + jnp.concatenate([mask, mask], axis=1)
        dots = dot(v_ref[region, :], g_wide, NT)
        exponent = jnp.exp(scores - jnp.max(scores, axis=0, keepdims=True))
        inverse = 1.0 / jnp.sum(exponent, axis=0, keepdims=True)
        attn = exponent * inverse
        delta = jnp.sum(attn * dots, axis=0, keepdims=True)
        dscore = (attn * (dots - delta)).astype(BF)
        dv = dot(attn.astype(BF), g_wide)
        dk = dot(dscore, q_wide)
        for part, at in halves:
            dv_ref[part, total, :] += dv[:, at]
            dk_ref[part, total, :] += dk[:, at]
        dq_wide = dot(dscore, k_ref[region, :], TN)
        head_col = lax.broadcasted_iota(jnp.int32, (queries, width), 1) // head_width
        dq = jnp.zeros((queries, width), F32)
        for head in range(GROUP):
            dq = jnp.where(head_col == head, dq_wide[head * queries : (head + 1) * queries], dq)
        dq_ref[mine, :] = (dq * head_width**-0.5).astype(BF)
        return carry

    lax.fori_loop(0, tiles, one_tile, 0)

    middle = (PAD_R + MARGIN) * KEY_COLS
    below = (PAD_R + MARGIN + band_rows) * KEY_COLS
    for part, acc in enumerate((dk_ref, dv_ref)):
        for lane, at in halves:
            for row in range(MARGIN):
                here = slice(row * band_cols, (row + 1) * band_cols)
                for start, out in ((PAD_R * KEY_COLS, top_ref), (below, bottom_ref)):
                    start = start + row * KEY_COLS
                    out[part, here, at] = acc[lane, start : start + band_cols, :].astype(BF)
            for pair in range(MARGIN):
                here = slice(edge + pair * 2 * EDGE_R, edge + (pair + 1) * 2 * EDGE_R)
                for start, out in ((0, top_ref), (below, bottom_ref)):
                    start = start + band_cols + 2 * pair
                    out[part, here, at] = jnp.concatenate(
                        [
                            acc[lane, pl.ds(start, EDGE_R, stride=KEY_COLS), :],
                            acc[lane, pl.ds(start + 1, EDGE_R, stride=KEY_COLS), :],
                        ],
                        axis=0,
                    ).astype(BF)
            for row in range(band_rows):
                base = middle + row * KEY_COLS
                mid_ref[part, row * band_cols : (row + 1) * band_cols, at] = acc[
                    lane, base : base + band_cols, :
                ].astype(BF)
            for col in range(MARGIN):
                here = slice(col * band_rows, (col + 1) * band_rows)
                start = middle + band_cols + col
                to_left_ref[part, here, at] = acc[
                    lane, pl.ds(start, band_rows, stride=KEY_COLS), :
                ].astype(BF)
                to_right_ref[part, here, at] = acc[
                    lane, pl.ds(start + MARGIN, band_rows, stride=KEY_COLS), :
                ].astype(BF)


def attention_grads(first, count, slots, start, masks, halo, qkv, grad_out, w_qkv, shape, before):
    band_rows, band_cols, total_rows = shape
    tokens, width = grad_out.shape
    head_width = width // HEADS
    block = GROUP * head_width
    groups = HEADS // GROUP
    region_tokens = (band_rows + 2 * MARGIN) * KEY_COLS
    total_tokens = (band_rows + 2 * MARGIN + 2 * PAD_R) * KEY_COLS
    side = MARGIN * band_rows
    edge = MARGIN * (band_cols + 2 * EDGE_R)
    corner = -(-2 * MARGIN * MARGIN // 16) * 16
    halo_tokens = 2 * (side + MARGIN * band_cols + corner)
    whole = lambda g: (0, 0)
    column = lambda offset: (lambda g: (0, offset + first + g))
    slot = lambda g: (0, 0, first % slots + g)
    halves = [(2, edge), (2, edge), (2, tokens), (2, side), (2, side)]
    out_shape = [jax.ShapeDtypeStruct((tokens, width), BF)] + [
        jax.ShapeDtypeStruct(s + (slots * block,), BF) for s in halves
    ]
    aliases = {}
    if before:
        aliases = {14 + i: place for i, (place, _) in enumerate(before)}
    return pl.pallas_call(
        functools.partial(
            attention_kernel, band_rows, band_cols, total_rows, head_width, len(before)
        ),
        grid=(count,),
        in_specs=[
            pl.BlockSpec(memory_space=pltpu.SMEM),
            pl.BlockSpec(masks.shape, lambda g: (0, 0, 0)),
        ]
        + [pl.BlockSpec(piece.shape, whole) for piece in halo]
        + [
            pl.BlockSpec((tokens, block), column(0)),
            pl.BlockSpec((tokens, block), column(groups)),
            pl.BlockSpec((tokens, block), column(2 * groups)),
            pl.BlockSpec((tokens, block), column(0)),
            pl.BlockSpec((width, block), column(groups)),
            pl.BlockSpec((width, block), column(2 * groups)),
        ]
        + [pl.BlockSpec(memory_space=pl.ANY)] * len(before),
        out_specs=[pl.BlockSpec((tokens, block), column(0))]
        + [pl.BlockSpec(s + (block,), slot) for s in halves],
        out_shape=out_shape,
        input_output_aliases=aliases,
        scratch_shapes=[
            pltpu.VMEM((halo_tokens, width), BF),
            pltpu.VMEM((block // LANES, (band_rows + 2 * MARGIN) * HALO_COLS, LANES), F32),
            pltpu.VMEM((tokens, block), BF),
            pltpu.VMEM((region_tokens, block), BF),
            pltpu.VMEM((region_tokens, block), BF),
            pltpu.VMEM((block // LANES, total_tokens, LANES), F32),
            pltpu.VMEM((block // LANES, total_tokens, LANES), F32),
        ],
        compiler_params=pltpu.CompilerParams(
            dimension_semantics=("arbitrary",), vmem_limit_bytes=44 * MIB
        ),
        cost_estimate=pl.CostEstimate(
            flops=count * 9 * 10**9, bytes_accessed=count * 8 * MIB, transcendentals=count * 10**6
        ),
    )(start, masks, *halo, qkv, qkv, qkv, grad_out, w_qkv, w_qkv, *[a for _, a in before])


def merge_kernel(band_rows, edge, left_ref, right_ref, above_ref, below_ref, ol_ref, or_ref):
    for part in range(2):
        for col in range(2 * MARGIN):
            source, target = (left_ref, ol_ref) if col < MARGIN else (right_ref, or_ref)
            base = (col % MARGIN) * band_rows
            pair = slice(edge + (col // 2) * 2 * EDGE_R, edge + (col // 2 + 1) * 2 * EDGE_R)
            odd = slice((col % 2) * EDGE_R, (col % 2 + 1) * EDGE_R)
            rows = source[part, base : base + band_rows, :].astype(F32)
            first = rows[:EDGE_R] + above_ref[part, pair, :].astype(F32)[odd]
            last = rows[band_rows - EDGE_R :] + below_ref[part, pair, :].astype(F32)[odd]
            target[part, base : base + band_rows, :] = jnp.concatenate(
                [first, rows[EDGE_R : band_rows - EDGE_R], last], axis=0
            ).astype(BF)


def merge_sides(left, right, above, below, band_rows, band_cols, block):
    width = left.shape[2]
    spec = lambda a: pl.BlockSpec((2, a.shape[1], block), lambda g: (0, 0, g))
    return pl.pallas_call(
        functools.partial(merge_kernel, band_rows, MARGIN * band_cols),
        grid=(width // block,),
        in_specs=[spec(left), spec(right), spec(above), spec(below)],
        out_specs=[spec(left), spec(right)],
        out_shape=[jax.ShapeDtypeStruct(left.shape, BF), jax.ShapeDtypeStruct(right.shape, BF)],
        cost_estimate=pl.CostEstimate(flops=10**6, bytes_accessed=4 * MIB, transcendentals=0),
    )(left, right, above, below)


def finish_kernel(band_rows, band_cols, own_ref, above_ref, below_ref, left_ref, right_ref, out_ref, acc_ref):
    edge = MARGIN * band_cols
    tokens = band_rows * band_cols
    for lane in range(acc_ref.shape[0]):
        at = slice(lane * LANES, (lane + 1) * LANES)
        acc_ref[lane] = own_ref[0, :, at].astype(F32)
        acc_ref[lane, :edge, :] += above_ref[0, :edge, at].astype(F32)
        acc_ref[lane, tokens - edge :, :] += below_ref[0, :edge, at].astype(F32)
        for col in range(MARGIN):
            here = slice(col * band_rows, (col + 1) * band_rows)
            first = pl.ds(col, band_rows, stride=band_cols)
            last = pl.ds(band_cols - MARGIN + col, band_rows, stride=band_cols)
            acc_ref[lane, first, :] += left_ref[0, here, at].astype(F32)
            acc_ref[lane, last, :] += right_ref[0, here, at].astype(F32)
        out_ref[:, at] = acc_ref[lane].astype(BF)


def finish(own, above, below, left, right, band_rows, band_cols, block):
    _, tokens, width = own.shape
    count = width // block
    spec = lambda a: pl.BlockSpec((1, a.shape[1], block), lambda p, g: (p, 0, g))
    return pl.pallas_call(
        functools.partial(finish_kernel, band_rows, band_cols),
        grid=(2, count),
        in_specs=[spec(a) for a in (own, above, below, left, right)],
        out_specs=pl.BlockSpec((tokens, block), lambda p, g: (0, p * count + g)),
        out_shape=jax.ShapeDtypeStruct((tokens, 2 * width), BF),
        scratch_shapes=[pltpu.VMEM((block // LANES, tokens, LANES), F32)],
        cost_estimate=pl.CostEstimate(flops=10**6, bytes_accessed=4 * MIB, transcendentals=0),
    )(own, above, below, left, right)


def shifted(array, axis, by, wrap):
    size = lax.axis_size(axis)
    route = [(i, (i + by) % size) for i in range(size) if wrap or 0 <= i + by < size]
    return lax.ppermute(array, axis, route)


def exchanged(array, axis, flip):
    return lax.ppermute(array, axis, [(i, i ^ flip) for i in range(lax.axis_size(axis))])


def bits_of(axis):
    return [(axis, 1 << b) for b in range((lax.axis_size(axis) - 1).bit_length())]


def feature_order(stages):
    n_lon, n_lat = lax.axis_size("lon"), lax.axis_size("lat")
    unit = {"lon": 1, "lat": n_lon, "dp": n_lon * n_lat}
    order = np.arange(n_lon)
    for axis, bit in reversed(stages):
        order = np.concatenate([order, order + unit[axis] * bit])
    return order.astype(np.int32)


def reduce_rows(rows, columns, stages, scale):
    half = rows.shape[0] // 2
    send = (dot(rows[half:], columns) * scale).astype(BF)
    keep = dot(rows[:half], columns) * scale
    axis, bit = stages[0]
    total = keep + exchanged(send, axis, bit).astype(F32)
    for axis, bit in stages[1:]:
        half = total.shape[0] // 2
        total = total[:half] + exchanged(total[half:].astype(BF), axis, bit).astype(F32)
    n_lon = lax.axis_size("lon")
    block = total.shape[0] // n_lon
    result = total[:block]
    for flip in range(1, n_lon):
        part = total[flip * block : (flip + 1) * block].astype(BF)
        result = result + exchanged(part, "lon", flip).astype(F32)
    return result


def body(inputs, grad_out, w_qkv):
    _, band_rows, band_cols, width = inputs.shape
    n_lat, n_lon, n_dp = lax.axis_size("lat"), lax.axis_size("lon"), lax.axis_size("dp")
    band_start = lax.axis_index("lat") * band_rows
    total_rows = band_rows * n_lat
    tokens = band_rows * band_cols
    block = GROUP * (width // HEADS)
    slots = HEADS // GROUP // 2
    shape = (band_rows, band_cols, total_rows)
    own = inputs.reshape(band_rows, band_cols, width)
    flat_inputs = inputs.reshape(tokens, width)
    flat_grad = grad_out.reshape(tokens, width)

    side = MARGIN * band_rows
    swap = lambda a: a.transpose(1, 0, 2).reshape(side, width)
    above = shifted(own[band_rows - MARGIN :], "lat", 1, False)
    below = shifted(own[:MARGIN], "lat", -1, False)
    left = shifted(swap(own[:, band_cols - MARGIN :]), "lon", 1, True)
    right = shifted(swap(own[:, :MARGIN]), "lon", -1, True)
    corner = 2 * MARGIN * MARGIN
    rims = jnp.stack([above, below])
    corner_left = shifted(rims[:, :, band_cols - MARGIN :].reshape(corner, width), "lon", 1, True)
    corner_right = shifted(rims[:, :, :MARGIN].reshape(corner, width), "lon", -1, True)
    above, below = above.reshape(-1, width), below.reshape(-1, width)
    halo = (left, right, above, below, corner_left, corner_right)

    start = band_start.reshape(1)
    masks = window_masks(start, band_rows, band_cols, total_rows)
    qkv = dot(flat_inputs, w_qkv).astype(BF)
    lat_bits = bits_of("lat")
    x_first = lat_bits[:1] + bits_of("dp") + lat_bits[1:]
    y_first = lat_bits + bits_of("dp")
    me = (lax.axis_index("dp") * n_lat + lax.axis_index("lat")) * n_lon + lax.axis_index("lon")
    blocks = flat_inputs.T.reshape(n_dp * n_lat * n_lon, -1, tokens)
    rows_x = blocks[me ^ feature_order(x_first)].reshape(width, tokens)
    rows_y = blocks[me ^ feature_order(y_first)].reshape(width, tokens)
    scale = float(tokens * n_dp * n_lat * n_lon) ** -0.5

    attend = lambda first, count, before: attention_grads(
        first, count, slots, start, masks, halo, qkv, flat_grad, w_qkv, shape, before
    )
    one = attend(0, slots, [])
    two = attend(slots, 1, [(0, one[0])])
    two = attend(slots + 1, 1, list(enumerate(two)))
    dq = two[0]

    pieces = []
    for _, top, bottom, mid, to_left, to_right in (one, two):
        from_below = shifted(top, "lat", -1, False)
        from_above = shifted(bottom, "lat", 1, False)
        to_left, to_right = merge_sides(
            to_left, to_right, from_above, from_below, band_rows, band_cols, block
        )
        from_right = shifted(to_left, "lon", -1, True)
        from_left = shifted(to_right, "lon", 1, True)
        pieces.append(
            finish(mid, from_above, from_below, from_left, from_right, band_rows, band_cols, block)
        )

    half = slots * block
    gw_q = reduce_rows(rows_x, dq, x_first, scale)
    gw_1 = reduce_rows(rows_y, pieces[0], y_first, scale)
    gw_2 = reduce_rows(rows_x, pieces[1], x_first, scale)
    grad_w = jnp.concatenate(
        [gw_q, gw_1[:, :half], gw_2[:, :half], gw_1[:, half:], gw_2[:, half:]], axis=1
    )
    grad_proj = jnp.concatenate(
        [dq, pieces[0][:, :half], pieces[1][:, :half], pieces[0][:, half:], pieces[1][:, half:]],
        axis=1,
    )
    grad_inputs = dot(grad_proj, w_qkv, NT).astype(BF).reshape(inputs.shape)
    return (grad_inputs, grad_w)


def solution(mesh):
    in_specs = (P("dp", "lat", "lon", None), P("dp", "lat", "lon", None), P())
    out_specs = (P("dp", "lat", "lon", None), P(("dp", "lat", "lon"), None))
    return jax.shard_map(body, mesh=mesh, in_specs=in_specs, out_specs=out_specs, check_vma=False)
```

time: 286 us -> 223 us (0.78)
  waiting for transfers between devices: 160 us -> 52.7 us
  starting transfers between devices: 20.9 us -> 51.7 us
  Pallas kernels: 40.9 us -> 58.6 us
  between operations: 14.2 us -> 1.16 us
  matrix products: 13.5 us -> 25.1 us
  other arithmetic: 10.5 us -> 4.2 us
    unnamed x2 -> x0, waiting for transfers between devices: 105 us -> none
    ppermute x8 -> x14, waiting for transfers between devices: 54.7 us -> 22.4 us  [shifted(): return lax.ppermute(array, axis, route)]
    ppermute x0 -> x18, waiting for transfers between devices: none -> 30.4 us  [exchanged(): lax.ppermute(array, axis, [(i, i ^ flip) for i in range(lax.axis_size(axi...]
    ppermute x0 -> x18, starting transfers between devices: none -> 22.2 us  [exchanged(): lax.ppermute(array, axis, [(i, i ^ flip) for i in range(lax.axis_size(axi...]
    pallas_call x0 -> x5, Pallas kernels: none -> 16.6 us  [the longest x2 8.59 us: finish(): pl.pallas_call(functools.partial(finish_kernel, band_rows, band_cols), gr...]
    dot_general x2 -> x8, matrix products: 13.5 us -> 25.1 us  [dot(): return lax.dot_general(a, b, dims, preferred_element_type=F32)]
    ppermute x8 -> x14, starting transfers between devices: 20.8 us -> 29.5 us  [shifted(): return lax.ppermute(array, axis, route)]
    reshape x2, local copies, waits for them, and re-layouts: 9.31 us -> 2.36 us  [the longest x1 1.65 us: body(): rims[:, :, :MARGIN].reshape(corner, width)]
  transfers between devices with their start and end apart: 9 -> 32, of which waited for: 7 -> 16; matrix products, arithmetic and copies ran while one was open for 6% -> 21% of each run, Pallas kernels for 0% -> 17%
where the time goes in v2:
time: 223 us; the launch traced here: 222 us
  Pallas kernels  58.6 us (26%)
  waiting for transfers between devices  52.7 us (24%)
  starting transfers between devices  51.7 us (23%)
  local copies, waits for them, and re-layouts  28.8 us (13%)
  matrix products  25.1 us (11%)
  other arithmetic  4.2 us (2%)
    pallas_call x3, Pallas kernels, attention_grads(): pl.pallas_call(functools.partial(attention_kernel, band_rows, band_cols,...  42.1 us
    ppermute x18, waiting for transfers between devices, exchanged(): lax.ppermute(array, axis, [(i, i ^ flip) for i in range(lax.axis_size(axi...  30.4 us
    ppermute x14, starting transfers between devices, shifted(): return lax.ppermute(array, axis, route)  29.5 us
    dot_general x8, matrix products, dot(): return lax.dot_general(a, b, dims, preferred_element_type=F32)  25.1 us
    ppermute x14, waiting for transfers between devices, shifted(): return lax.ppermute(array, axis, route)  22.4 us
    ppermute x18, starting transfers between devices, exchanged(): lax.ppermute(array, axis, [(i, i ^ flip) for i in range(lax.axis_size(axi...  22.2 us
    unnamed x73, local copies, waits for them, and re-layouts  14.1 us
    pallas_call x2, Pallas kernels, finish(): pl.pallas_call(functools.partial(finish_kernel, band_rows, band_cols), gr...  8.59 us
  transfers between devices with their start and end apart: 32, of which 16 were waited for; matrix products, arithmetic and copies ran while one was open for 21% of the time, Pallas kernels for 17%

profile of v2, /device:TPU:0, one launch (start us, length us, event | category | flops | bytes accessed | tf_op | source)
XLA Modules:
  0.0 222.3 jit_solution(5204105101229288661)
XLA Ops:
  3.9 3.0 %collective-permute-start.2 = (bf16[6,16,1024]{2,1,0:T(8,128)(2,1)}, bf16[6,16,1024]{2,1,0:T(8,128)(2,1)S(1)}, u32[]{:S(2)}, u32[]{:S(2)}) collective-permute-start(bf16[6,16,1024]{2,1,0:T(8,128)(2,1)} %get-tuple-element.57), channel_id=1, source_target_pairs={{0,4},{4,8},{8,12},{1,5},{5,9},{9,13},{2,6},{6,10},{10,14},{3,7},{... | collective-permute-start | bytes 589832 | tf_op jit(solution)/shard_map/ppermute | solution.py:348
  9.3 3.0 %collective-permute-start = (bf16[192,1024]{1,0:T(8,128)(2,1)}, bf16[192,1024]{1,0:T(8,128)(2,1)S(1)}, u32[]{:S(2)}, u32[]{:S(2)}) collective-permute-start(bf16[192,1024]{1,0:T(8,128)(2,1)} %bitcast.3), channel_id=1, source_target_pairs={{0,1},{1,2},{2,3},{3,0},{4,5},{5,6},{6,7},{7,4},{8,9},{9,10},{10,1... | collective-permute-start | bytes 1179656 | tf_op jit(solution)/shard_map/ppermute | solution.py:348
  17.5 7.7 %convolution_convert_fusion.refs_8_.refs_9_.refs_10_ = bf16[512,3072]{1,0:T(8,128)(2,1)} fusion(bf16[512,1024]{1,0:T(8,128)(2,1)S(1)} %bitcast.57, bf16[1024,3072]{1,0:T(8,128)(2,1)} %refs_13_.5), kind=kOutput, calls=%fused_computation.2 | convolution fusion | flops 3222798336 | bytes 10485760 | tf_op jit(solution)/shard_map/dot_general | solution.py:33
  27.9 3.3 %shard_map.68.refs_1_ = bf16[8,512,128]{2,1,0:T(8,128)(2,1)} custom-call(s32[1]{0:T(128)} %bitcast.start_ref.refs_0_), custom_call_target="tpu_custom_call" | custom-call | flops 10000000 | bytes 2097152 | tf_op jit(solution)/shard_map/pallas_call | solution.py:67
  34.3 3.8 %collective-permute-start.5 = (bf16[72,1024]{1,0:T(8,128)(2,1)}, bf16[72,1024]{1,0:T(8,128)(2,1)S(1)}, u32[]{:S(2)}, u32[]{:S(2)}) collective-permute-start(bf16[72,1024]{1,0:T(8,128)(2,1)} %reshape.55), channel_id=1, source_target_pairs={{0,3},{1,0},{2,1},{3,2},{4,7},{5,4},{6,5},{7,6},{8,11},{9,8},{10,9... | collective-permute-start | bytes 442376 | tf_op jit(solution)/shard_map/ppermute | solution.py:348
  39.2 3.9 %collective-permute-done.4.refs_6_ = bf16[72,1024]{1,0:T(8,128)(2,1)S(1)} collective-permute-done((bf16[72,1024]{1,0:T(8,128)(2,1)}, bf16[72,1024]{1,0:T(8,128)(2,1)S(1)}, u32[]{:S(2)}, u32[]{:S(2)}) %collective-permute-start.4) | collective-permute-done | bytes 147488 | tf_op jit(solution)/shard_map/ppermute | solution.py:348
  47.7 19.9 %shard_map.69 = (bf16[512,1024]{1,0:T(8,128)(2,1)S(1)}, bf16[2,192,512]{2,1,0:T(8,128)(2,1)S(1)}, bf16[2,192,512]{2,1,0:T(8,128)(2,1)S(1)}, bf16[2,512,512]{2,1,...) custom-call(s32[1]{0:T(128)} %bitcast.start_ref.refs_0_, ...), custom_call_target="tpu_custom_call" | custom-call | flops 17999998976 | bytes 16777216 | tf_op jit(solution)/shard_map/pallas_call | solution.py:244
  74.9 11.0 %shard_map.70 = (bf16[512,1024]{1,0:T(8,128)(2,1)S(1)}, bf16[2,192,512]{2,1,0:T(8,128)(2,1)}, bf16[2,192,512]{2,1,0:T(8,128)(2,1)}, bf16[2,512,512]{2,1,0:T(8,12...) custom-call(s32[1]{0:T(128)} %bitcast.start_ref.refs_0_, ...), custom_call_target="tpu_custom_call", output_to_operand_aliasing={{0}: (14, {})} | custom-call | flops 8999999488 | bytes 8388608 | tf_op jit(solution)/shard_map/pallas_call | solution.py:244
  86.0 11.1 %shard_map.71 = (bf16[512,1024]{1,0:T(8,128)(2,1)S(1)}, bf16[2,192,512]{2,1,0:T(8,128)(2,1)}, bf16[2,192,512]{2,1,0:T(8,128)(2,1)}, bf16[2,512,512]{2,1,0:T(8,12...) custom-call(s32[1]{0:T(128)} %bitcast.start_ref.refs_0_, ...), custom_call_target="tpu_custom_call", output_to_operand_aliasing={{0}: (14, {}), {1}: (15, {}), {2}: (16, {}), {3}: (17, {}),... | custom-call | flops 8999999488 | bytes 8388608 | tf_op jit(solution)/shard_map/pallas_call | solution.py:244
  97.9 3.8 %collective-permute-start.10 = (bf16[2,192,512]{2,1,0:T(8,128)(2,1)}, bf16[2,192,512]{2,1,0:T(8,128)(2,1)}, u32[]{:S(2)}, u32[]{:S(2)}) collective-permute-start(bf16[2,192,512]{2,1,0:T(8,128)(2,1)} %get-tuple-element.40), channel_id=1, source_target_pairs={{0,4},{4,8},{8,12},{1,5},{5,9},{9,13},{2,6},{6,10},{10,14},{3,7},{... | collective-permute-start | bytes 1179656 | tf_op jit(solution)/shard_map/ppermute | solution.py:348
  110.7 3.2 %collective-permute-start.9 = (bf16[2,192,512]{2,1,0:T(8,128)(2,1)}, bf16[2,192,512]{2,1,0:T(8,128)(2,1)}, u32[]{:S(2)}, u32[]{:S(2)}) collective-permute-start(bf16[2,192,512]{2,1,0:T(8,128)(2,1)} %get-tuple-element.38), channel_id=1, source_target_pairs={{0,3},{1,0},{2,1},{3,2},{4,7},{5,4},{6,5},{7,6},{8,11},{9,8},{10,9... | collective-permute-start | bytes 1179656 | tf_op jit(solution)/shard_map/ppermute | solution.py:348
  118.0 3.8 %collective-permute-start.13 = (bf16[2,192,512]{2,1,0:T(8,128)(2,1)}, bf16[2,192,512]{2,1,0:T(8,128)(2,1)}, u32[]{:S(2)}, u32[]{:S(2)}) collective-permute-start(bf16[2,192,512]{2,1,0:T(8,128)(2,1)} %get-tuple-element.45), channel_id=1, source_target_pairs={{0,3},{1,0},{2,1},{3,2},{4,7},{5,4},{6,5},{7,6},{8,11},{9,8},{10,9... | collective-permute-start | bytes 1179656 | tf_op jit(solution)/shard_map/ppermute | solution.py:348
  124.1 8.2 %collective-permute-done.9.right_ref = bf16[2,192,512]{2,1,0:T(8,128)(2,1)} collective-permute-done((bf16[2,192,512]{2,1,0:T(8,128)(2,1)}, bf16[2,192,512]{2,1,0:T(8,128)(2,1)}, u32[]{:S(2)}, u32[]{:S(2)}) %collective-permute-start.9) | collective-permute-done | bytes 393248 | tf_op jit(solution)/shard_map/ppermute | solution.py:348
  132.2 4.3 %shard_map.73 = bf16[512,1024]{1,0:T(8,128)(2,1)} custom-call(bf16[2,512,512]{2,1,0:T(8,128)(2,1)} %copy-done, bf16[2,192,512]{2,1,0:T(8,128)(2,1)} %copy-done.24, bf16[2,192,512]{2,1,0:T(8,128)(2,1)} %copy-done.25, bf16[2,192,512]{2,1,0:T(8,128)(2,1)} %copy-done.28, bf16[2,192,512]{2,1,0:T(8,128)(2,1)} %collective-permute-done.9.right_ref), custom_call_target="tpu_custom_call" | custom-call | flops 1000000 | bytes 4194304 | tf_op jit(solution)/shard_map/pallas_call | solution.py:334
  136.6 2.9 %multiply_convert_fusion.1 = bf16[512,1024]{1,0:T(8,128)(2,1)} fusion(bf16[512,512]{1,0:T(8,128)(2,1)S(1)} %bitcast.63, bf16[512,1024]{1,0:T(8,128)(2,1)} %shard_map.73), kind=kOutput, calls=%fused_computation.6 | convolution fusion | flops 537919488 | bytes 2621440 | tf_op jit(solution)/shard_map/dot_general | solution.py:33
  141.1 6.3 %collective-permute-done.13.right_ref = bf16[2,192,512]{2,1,0:T(8,128)(2,1)} collective-permute-done((bf16[2,192,512]{2,1,0:T(8,128)(2,1)}, bf16[2,192,512]{2,1,0:T(8,128)(2,1)}, u32[]{:S(2)}, u32[]{:S(2)}) %collective-permute-start.13) | collective-permute-done | bytes 393248 | tf_op jit(solution)/shard_map/ppermute | solution.py:348
  147.4 4.3 %shard_map.75 = bf16[512,1024]{1,0:T(8,128)(2,1)} custom-call(bf16[2,512,512]{2,1,0:T(8,128)(2,1)} %copy-done.1, bf16[2,192,512]{2,1,0:T(8,128)(2,1)} %collective-permute-done.10.above_ref, bf16[2,192,512]{2,1,0:T(8,128)(2,1)} %collective-permute-done.11.below_ref, bf16[2,192,512]{2,1,0:T(8,128)(2,1)} %collective-permute-done.12.left_ref, ...), custom_call_target="tpu_custom_call" | custom-call | flops 1000000 | bytes 4194304 | tf_op jit(solution)/shard_map/pallas_call | solution.py:334
  160.8 7.4 %convolution_convert_fusion.1 = bf16[512,1024]{1,0:T(8,128)(2,1)} fusion(bf16[512,3072]{1,0:T(8,128)(2,1)S(1)} %copy-done.29, bf16[1024,3072]{1,0:T(8,128)(2,1)} %refs_13_.5), kind=kOutput, calls=%fused_computation.9 | convolution fusion | flops 3221749760 | bytes 10485760 | tf_op jit(solution)/shard_map/dot_general | solution.py:33
  168.9 4.9 %collective-permute-done.15 = bf16[256,1024]{1,0:T(8,128)(2,1)S(1)} collective-permute-done((bf16[256,1024]{1,0:T(8,128)(2,1)S(1)}, bf16[256,1024]{1,0:T(8,128)(2,1)S(1)}, u32[]{:S(2)}, u32[]{:S(2)}) %collective-permute-start.15) | collective-permute-done | bytes 524320 | tf_op jit(solution)/shard_map/ppermute | solution.py:352
  176.9 5.4 %collective-permute-done.16 = bf16[128,1024]{1,0:T(8,128)(2,1)S(1)} collective-permute-done((bf16[128,1024]{1,0:T(8,128)(2,1)S(1)}, bf16[128,1024]{1,0:T(8,128)(2,1)S(1)}, u32[]{:S(2)}, u32[]{:S(2)}) %collective-permute-start.16) | collective-permute-done | bytes 262176 | tf_op jit(solution)/shard_map/ppermute | solution.py:352
  192.4 6.4 %collective-permute-done.21 = bf16[256,1024]{1,0:T(8,128)(2,1)S(1)} collective-permute-done((bf16[256,1024]{1,0:T(8,128)(2,1)S(1)}, bf16[256,1024]{1,0:T(8,128)(2,1)S(1)}, u32[]{:S(2)}, u32[]{:S(2)}) %collective-permute-start.21) | collective-permute-done | bytes 524320 | tf_op jit(solution)/shard_map/ppermute | solution.py:352
  202.3 3.8 %collective-permute-done.22 = bf16[128,1024]{1,0:T(8,128)(2,1)S(1)} collective-permute-done((bf16[128,1024]{1,0:T(8,128)(2,1)S(1)}, bf16[128,1024]{1,0:T(8,128)(2,1)S(1)}, u32[]{:S(2)}, u32[]{:S(2)}) %collective-permute-start.22) | collective-permute-done | bytes 262176 | tf_op jit(solution)/shard_map/ppermute | solution.py:352
  210.6 2.8 %collective-permute-start.29 = (bf16[32,1024]{1,0:T(8,128)(2,1)S(1)}, bf16[32,1024]{1,0:T(8,128)(2,1)S(1)}, u32[]{:S(2)}, u32[]{:S(2)}) collective-permute-start(bf16[32,1024]{1,0:T(8,128)(2,1)S(1)} %get-tuple-element.62), channel_id=1, source_target_pairs={{0,1},{1,0},{2,3},{3,2},{4,5},{5,4},{6,7},{7,6},{8,9},{9,8},{10,11... | collective-permute-start | bytes 196616 | tf_op jit(solution)/shard_map/ppermute | solution.py:352
  215.3 3.2 %collective-permute-done.24 = bf16[32,1024]{1,0:T(8,128)(2,1)S(1)} collective-permute-done((bf16[32,1024]{1,0:T(8,128)(2,1)S(1)}, bf16[32,1024]{1,0:T(8,128)(2,1)S(1)}, u32[]{:S(2)}, u32[]{:S(2)}) %collective-permute-start.24) | collective-permute-done | bytes 65568 | tf_op jit(solution)/shard_map/ppermute | solution.py:352
  (167 shorter events, 83.5 us)
Async XLA Ops:
  2.4 28.7 %collective-permute-start.3 = (bf16[6,16,1024]{2,1,0:T(8,128)(2,1)}, bf16[6,16,1024]{2,1,0:T(8,128)(2,1)S(1)}, u32[]{:S(2)}, u32[]{:S(2)}) collective-permute-start(bf16[6,16,1024]{2,1,0:T(8,128)(2,1)} %get-tuple-element.56), channel_id=1, source_target_pairs={{4,0},{8,4},{12,8},{5,1},{9,5},{13,9},{6,2},{10,6},{14,10},{7,3},{... | collective-permute-start | bytes 589832 | tf_op jit(solution)/shard_map/ppermute | solution.py:348
  3.9 27.3 %collective-permute-start.2 = (bf16[6,16,1024]{2,1,0:T(8,128)(2,1)}, bf16[6,16,1024]{2,1,0:T(8,128)(2,1)S(1)}, u32[]{:S(2)}, u32[]{:S(2)}) collective-permute-start(bf16[6,16,1024]{2,1,0:T(8,128)(2,1)} %get-tuple-element.57), channel_id=1, source_target_pairs={{0,4},{4,8},{8,12},{1,5},{5,9},{9,13},{2,6},{6,10},{10,14},{3,7},{... | collective-permute-start | bytes 589832 | tf_op jit(solution)/shard_map/ppermute | solution.py:348
  9.3 35.0 %collective-permute-start = (bf16[192,1024]{1,0:T(8,128)(2,1)}, bf16[192,1024]{1,0:T(8,128)(2,1)S(1)}, u32[]{:S(2)}, u32[]{:S(2)}) collective-permute-start(bf16[192,1024]{1,0:T(8,128)(2,1)} %bitcast.3), channel_id=1, source_target_pairs={{0,1},{1,2},{2,3},{3,0},{4,5},{5,6},{6,7},{7,4},{8,9},{9,10},{10,1... | collective-permute-start | bytes 1179656 | tf_op jit(solution)/shard_map/ppermute | solution.py:348
  13.3 31.0 %collective-permute-start.1 = (bf16[192,1024]{1,0:T(8,128)(2,1)}, bf16[192,1024]{1,0:T(8,128)(2,1)S(1)}, u32[]{:S(2)}, u32[]{:S(2)}) collective-permute-start(bf16[192,1024]{1,0:T(8,128)(2,1)} %bitcast.5), channel_id=1, source_target_pairs={{0,3},{1,0},{2,1},{3,2},{4,7},{5,4},{6,5},{7,6},{8,11},{9,8},{10,9... | collective-permute-start | bytes 1179656 | tf_op jit(solution)/shard_map/ppermute | solution.py:348
  34.3 8.8 %collective-permute-start.4 = (bf16[72,1024]{1,0:T(8,128)(2,1)}, bf16[72,1024]{1,0:T(8,128)(2,1)S(1)}, u32[]{:S(2)}, u32[]{:S(2)}) collective-permute-start(bf16[72,1024]{1,0:T(8,128)(2,1)} %reshape.54), channel_id=1, source_target_pairs={{0,1},{1,2},{2,3},{3,0},{4,5},{5,6},{6,7},{7,4},{8,9},{9,10},{10,1... | collective-permute-start | bytes 442376 | tf_op jit(solution)/shard_map/ppermute | solution.py:348
  34.3 10.0 %collective-permute-start.5 = (bf16[72,1024]{1,0:T(8,128)(2,1)}, bf16[72,1024]{1,0:T(8,128)(2,1)S(1)}, u32[]{:S(2)}, u32[]{:S(2)}) collective-permute-start(bf16[72,1024]{1,0:T(8,128)(2,1)} %reshape.55), channel_id=1, source_target_pairs={{0,3},{1,0},{2,1},{3,2},{4,7},{5,4},{6,5},{7,6},{8,11},{9,8},{10,9... | collective-permute-start | bytes 442376 | tf_op jit(solution)/shard_map/ppermute | solution.py:348
  67.7 38.4 %collective-permute-start.6 = (bf16[2,192,512]{2,1,0:T(8,128)(2,1)S(1)}, bf16[2,192,512]{2,1,0:T(8,128)(2,1)S(1)}, u32[]{:S(2)}, u32[]{:S(2)}) collective-permute-start(bf16[2,192,512]{2,1,0:T(8,128)(2,1)S(1)} %get-tuple-element.33), channel_id=1, source_target_pairs={{0,4},{4,8},{8,12},{1,5},{5,9},{9,13},{2,6},{6,10},{10,14},{3,7},{... | collective-permute-start | bytes 1179656 | tf_op jit(solution)/shard_map/ppermute | solution.py:348
  69.6 36.5 %collective-permute-start.7 = (bf16[2,192,512]{2,1,0:T(8,128)(2,1)S(1)}, bf16[2,192,512]{2,1,0:T(8,128)(2,1)S(1)}, u32[]{:S(2)}, u32[]{:S(2)}) collective-permute-start(bf16[2,192,512]{2,1,0:T(8,128)(2,1)S(1)} %get-tuple-element.34), channel_id=1, source_target_pairs={{4,0},{8,4},{12,8},{5,1},{9,5},{13,9},{6,2},{10,6},{14,10},{7,3},{... | collective-permute-start | bytes 1179656 | tf_op jit(solution)/shard_map/ppermute | solution.py:348
  97.9 17.7 %collective-permute-start.10 = (bf16[2,192,512]{2,1,0:T(8,128)(2,1)}, bf16[2,192,512]{2,1,0:T(8,128)(2,1)}, u32[]{:S(2)}, u32[]{:S(2)}) collective-permute-start(bf16[2,192,512]{2,1,0:T(8,128)(2,1)} %get-tuple-element.40), channel_id=1, source_target_pairs={{0,4},{4,8},{8,12},{1,5},{5,9},{9,13},{2,6},{6,10},{10,14},{3,7},{... | collective-permute-start | bytes 1179656 | tf_op jit(solution)/shard_map/ppermute | solution.py:348
  101.7 13.9 %collective-permute-start.11 = (bf16[2,192,512]{2,1,0:T(8,128)(2,1)}, bf16[2,192,512]{2,1,0:T(8,128)(2,1)}, u32[]{:S(2)}, u32[]{:S(2)}) collective-permute-start(bf16[2,192,512]{2,1,0:T(8,128)(2,1)} %get-tuple-element.41), channel_id=1, source_target_pairs={{4,0},{8,4},{12,8},{5,1},{9,5},{13,9},{6,2},{10,6},{14,10},{7,3},{... | collective-permute-start | bytes 1179656 | tf_op jit(solution)/shard_map/ppermute | solution.py:348
  104.8 52.8 %collective-permute-start.14 = (bf16[512,1024]{1,0:T(8,128)(2,1)}, bf16[512,1024]{1,0:T(8,128)(2,1)}, u32[]{:S(2)}, u32[]{:S(2)}) collective-permute-start(bf16[512,1024]{1,0:T(8,128)(2,1)} %multiply_convert_fusion.2), channel_id=1, source_target_pairs={{0,4},{4,0},{8,12},{12,8},{1,5},{5,1},{9,13},{13,9},{2,6},{6,2},{1... | collective-permute-start | bytes 3145736 | tf_op jit(solution)/shard_map/ppermute | solution.py:352
  110.0 14.1 %collective-permute-start.8 = (bf16[2,192,512]{2,1,0:T(8,128)(2,1)}, bf16[2,192,512]{2,1,0:T(8,128)(2,1)S(1)}, u32[]{:S(2)}, u32[]{:S(2)}) collective-permute-start(bf16[2,192,512]{2,1,0:T(8,128)(2,1)} %get-tuple-element.37), channel_id=1, source_target_pairs={{0,1},{1,2},{2,3},{3,0},{4,5},{5,6},{6,7},{7,4},{8,9},{9,10},{10,1... | collective-permute-start | bytes 1179656 | tf_op jit(solution)/shard_map/ppermute | solution.py:348
  110.7 21.6 %collective-permute-start.9 = (bf16[2,192,512]{2,1,0:T(8,128)(2,1)}, bf16[2,192,512]{2,1,0:T(8,128)(2,1)}, u32[]{:S(2)}, u32[]{:S(2)}) collective-permute-start(bf16[2,192,512]{2,1,0:T(8,128)(2,1)} %get-tuple-element.38), channel_id=1, source_target_pairs={{0,3},{1,0},{2,1},{3,2},{4,7},{5,4},{6,5},{7,6},{8,11},{9,8},{10,9... | collective-permute-start | bytes 1179656 | tf_op jit(solution)/shard_map/ppermute | solution.py:348
  118.0 23.1 %collective-permute-start.12 = (bf16[2,192,512]{2,1,0:T(8,128)(2,1)}, bf16[2,192,512]{2,1,0:T(8,128)(2,1)}, u32[]{:S(2)}, u32[]{:S(2)}) collective-permute-start(bf16[2,192,512]{2,1,0:T(8,128)(2,1)} %get-tuple-element.44), channel_id=1, source_target_pairs={{0,1},{1,2},{2,3},{3,0},{4,5},{5,6},{6,7},{7,4},{8,9},{9,10},{10,1... | collective-permute-start | bytes 1179656 | tf_op jit(solution)/shard_map/ppermute | solution.py:348
  118.0 29.4 %collective-permute-start.13 = (bf16[2,192,512]{2,1,0:T(8,128)(2,1)}, bf16[2,192,512]{2,1,0:T(8,128)(2,1)}, u32[]{:S(2)}, u32[]{:S(2)}) collective-permute-start(bf16[2,192,512]{2,1,0:T(8,128)(2,1)} %get-tuple-element.45), channel_id=1, source_target_pairs={{0,3},{1,0},{2,1},{3,2},{4,7},{5,4},{6,5},{7,6},{8,11},{9,8},{10,9... | collective-permute-start | bytes 1179656 | tf_op jit(solution)/shard_map/ppermute | solution.py:348
  139.5 46.5 %collective-permute-start.20 = (bf16[512,1024]{1,0:T(8,128)(2,1)}, bf16[512,1024]{1,0:T(8,128)(2,1)S(1)}, u32[]{:S(2)}, u32[]{:S(2)}) collective-permute-start(bf16[512,1024]{1,0:T(8,128)(2,1)} %multiply_convert_fusion.1), channel_id=1, source_target_pairs={{0,4},{4,0},{8,12},{12,8},{1,5},{5,1},{9,13},{13,9},{2,6},{6,2},{1... | collective-permute-start | bytes 3145736 | tf_op jit(solution)/shard_map/ppermute | solution.py:352
  153.9 34.5 %collective-permute-start.26 = (bf16[512,1024]{1,0:T(8,128)(2,1)S(1)}, bf16[512,1024]{1,0:T(8,128)(2,1)S(1)}, u32[]{:S(2)}, u32[]{:S(2)}) collective-permute-start(bf16[512,1024]{1,0:T(8,128)(2,1)S(1)} %multiply_convert_fusion), channel_id=1, source_target_pairs={{0,4},{4,0},{8,12},{12,8},{1,5},{5,1},{9,13},{13,9},{2,6},{6,2},{1... | collective-permute-start | bytes 3145736 | tf_op jit(solution)/shard_map/ppermute | solution.py:352
  159.4 14.4 %collective-permute-start.15 = (bf16[256,1024]{1,0:T(8,128)(2,1)S(1)}, bf16[256,1024]{1,0:T(8,128)(2,1)S(1)}, u32[]{:S(2)}, u32[]{:S(2)}) collective-permute-start(bf16[256,1024]{1,0:T(8,128)(2,1)S(1)} %slice.302), channel_id=1, source_target_pairs={{0,16},{16,0},{1,17},{17,1},{2,18},{18,2},{3,19},{19,3},{4,20},{20... | collective-permute-start | bytes 1572872 | tf_op jit(solution)/shard_map/ppermute | solution.py:352
  174.0 8.3 %collective-permute-start.16 = (bf16[128,1024]{1,0:T(8,128)(2,1)S(1)}, bf16[128,1024]{1,0:T(8,128)(2,1)S(1)}, u32[]{:S(2)}, u32[]{:S(2)}) collective-permute-start(bf16[128,1024]{1,0:T(8,128)(2,1)S(1)} %slice.305), channel_id=1, source_target_pairs={{0,8},{4,12},{8,0},{12,4},{1,9},{5,13},{9,1},{13,5},{2,10},{6,14},... | collective-permute-start | bytes 786440 | tf_op jit(solution)/shard_map/ppermute | solution.py:352
  186.5 12.2 %collective-permute-start.21 = (bf16[256,1024]{1,0:T(8,128)(2,1)S(1)}, bf16[256,1024]{1,0:T(8,128)(2,1)S(1)}, u32[]{:S(2)}, u32[]{:S(2)}) collective-permute-start(bf16[256,1024]{1,0:T(8,128)(2,1)S(1)} %slice.301), channel_id=1, source_target_pairs={{0,8},{4,12},{8,0},{12,4},{1,9},{5,13},{9,1},{13,5},{2,10},{6,14},... | collective-permute-start | bytes 1572872 | tf_op jit(solution)/shard_map/ppermute | solution.py:352
  188.9 13.1 %collective-permute-start.27 = (bf16[256,1024]{1,0:T(8,128)(2,1)S(1)}, bf16[256,1024]{1,0:T(8,128)(2,1)S(1)}, u32[]{:S(2)}, u32[]{:S(2)}) collective-permute-start(bf16[256,1024]{1,0:T(8,128)(2,1)S(1)} %slice.300), channel_id=1, source_target_pairs={{0,16},{16,0},{1,17},{17,1},{2,18},{18,2},{3,19},{19,3},{4,20},{20... | collective-permute-start | bytes 1572872 | tf_op jit(solution)/shard_map/ppermute | solution.py:352
  202.2 8.3 %collective-permute-start.28 = (bf16[128,1024]{1,0:T(8,128)(2,1)S(1)}, bf16[128,1024]{1,0:T(8,128)(2,1)S(1)}, u32[]{:S(2)}, u32[]{:S(2)}) collective-permute-start(bf16[128,1024]{1,0:T(8,128)(2,1)S(1)} %slice.303), channel_id=1, source_target_pairs={{0,8},{4,12},{8,0},{12,4},{1,9},{5,13},{9,1},{13,5},{2,10},{6,14},... | collective-permute-start | bytes 786440 | tf_op jit(solution)/shard_map/ppermute | solution.py:352
  206.3 8.7 %collective-permute-start.23 = (bf16[32,1024]{1,0:T(8,128)(2,1)S(1)}, bf16[32,1024]{1,0:T(8,128)(2,1)S(1)}, u32[]{:S(2)}, u32[]{:S(2)}) collective-permute-start(bf16[32,1024]{1,0:T(8,128)(2,1)S(1)} %get-tuple-element.65), channel_id=1, source_target_pairs={{0,1},{1,0},{2,3},{3,2},{4,5},{5,4},{6,7},{7,6},{8,9},{9,8},{10,11... | collective-permute-start | bytes 196616 | tf_op jit(solution)/shard_map/ppermute | solution.py:352
  210.4 8.1 %collective-permute-start.24 = (bf16[32,1024]{1,0:T(8,128)(2,1)S(1)}, bf16[32,1024]{1,0:T(8,128)(2,1)S(1)}, u32[]{:S(2)}, u32[]{:S(2)}) collective-permute-start(bf16[32,1024]{1,0:T(8,128)(2,1)S(1)} %get-tuple-element.67), channel_id=1, source_target_pairs={{0,2},{1,3},{2,0},{3,1},{4,6},{5,7},{6,4},{7,5},{8,10},{9,11},{10,... | collective-permute-start | bytes 196616 | tf_op jit(solution)/shard_map/ppermute | solution.py:352
  (41 other events, 397.5 us)
